TPU v7x, 512 devices: a whole 4x8x8 slice. The times are simulated.
512 devices in a mesh: dp: 512 (over x, z, y, core).
Axes of the slice: x: 4, y: 8, z: 8, core: 2. Of those that a mesh axis runs over, the one named last changes fastest.
Arguments:
- sketch: bfloat16 [262144, 2048], P('dp'), may hold values from -5 to 5
- lanczos_basis: float32 [8, 262144], P(None, 'dp'), may hold values from -9 to 9
Outputs:
- gram_rows: bfloat16 [262144, 2560], P('dp')
- next_vector: float32 [262144], P('dp')
- coefficients: float32 [9], replicated
All inputs are finite; a program needn't handle non-finite values.
Results may differ from a plain program's by a relative error of at most 0.0042.
Values may be sent and summed in bfloat16 or wider, within the bound.
No kernel may reach another device: no remote copies, remote signals or barrier semaphores. Data moves between devices by JAX's collectives and lax.ppermute only.
A program may use at most 64 MiB of HBM per device.

v0:
```python
import jax
import jax.numpy as jnp
from jax import lax
from jax.sharding import PartitionSpec as P


def shifted(block, axis, distance):
    devices = range(lax.axis_size(axis))
    route = [((i - distance) % len(devices), i) for i in devices]
    return lax.ppermute(block, axis, route)


def pair_block(left_rows, right_rows):
    return lax.dot_general(
        left_rows, right_rows, (((1,), (1,)), ((), ())), preferred_element_type=jnp.float32
    ).astype(jnp.bfloat16)


def on_device(sketch, lanczos_basis):
    devices = lax.axis_size("dp")
    row_count = sketch.shape[0]
    total_rows = row_count * devices
    current = lanczos_basis[lanczos_basis.shape[0] - 1].astype(jnp.bfloat16)
    own_block = pair_block(sketch, sketch)
    band_list = [own_block]
    image_vec = jnp.dot(own_block, current, preferred_element_type=jnp.float32)
    for offset in (1, devices // 4):
        ahead_rows, ahead_vec = shifted((sketch, current), "dp", -offset)
        ahead_block = pair_block(sketch, ahead_rows)
        returned, behind_vec = shifted((ahead_block, current), "dp", offset)
        behind_block = returned.T
        image_vec = image_vec + jnp.dot(ahead_block, ahead_vec, preferred_element_type=jnp.float32)
        image_vec = image_vec + jnp.dot(
            behind_block, behind_vec, preferred_element_type=jnp.float32
        )
        band_list = band_list + [ahead_block, behind_block]
    gram_rows = jnp.concatenate(band_list, axis=1)
    partial_value = jnp.dot(lanczos_basis, image_vec, precision=lax.Precision.HIGHEST)
    coeffs = lax.psum(partial_value, "dp") / total_rows
    remainder = image_vec - jnp.dot(coeffs, lanczos_basis, precision=lax.Precision.HIGHEST)
    square_sum = lax.psum(jnp.sum(remainder * remainder), "dp")
    beta_value = jnp.sqrt(square_sum / total_rows + 1e-06)
    next_vector = remainder / beta_value
    coefficients = jnp.concatenate([coeffs, beta_value[None]])
    return (gram_rows, next_vector, coefficients)


def solution(mesh):
    placed = (P("dp", None), P(None, "dp"))
    return jax.shard_map(
        on_device,
        mesh=mesh,
        in_specs=placed,
        out_specs=(P("dp", None), P("dp"), P()),
        check_vma=False,
    )
```

profile of v0, /device:TPU:6, one launch (start us, length us, event | category | flops | bytes accessed | tf_op | source)
XLA Modules:
  0.0 307.9 jit_solution(591476355524702252)
XLA Ops:
  0.6 13.6 %collective-permute-start = (bf16[512,2048]{1,0:T(8,128)(2,1)}, bf16[512,2048]{1,0:T(8,128)(2,1)S(1)}, u32[]{:S(2)}, u32[]{:S(2)}) collective-permute-start(bf16[512,2048]{1,0:T(8,128)(2,1)} %param.2), channel_id=1, source_target_pairs={{1,0},{2,1},{3,2},{4,3},{5,4},{6,5},{7,6},{8,7},{9,8},{10,9},{11,1... | collective-permute-start | bytes 6291464 | tf_op jit(solution)/shard_map/ppermute | solution.py:10
  14.2 2.4 collective-permute-start.2
  16.7 0.7 fusion.6
  17.4 0.0 copy-start.4
  17.4 0.0 copy-start.5
  17.4 2.1 collective-permute-start.5
  19.5 4.6 %collective-permute-start.7 = (bf16[512]{0:T(512)(128)(2,1)S(1)}, bf16[512]{0:T(512)(128)(2,1)S(1)}, u32[]{:S(2)}, u32[]{:S(2)}) collective-permute-start(bf16[512]{0:T(512)(128)(2,1)S(1)} %fusion.6), channel_id=1, source_target_pairs={{384,0},{385,1},{386,2},{387,3},{388,4},{389,5},{390,6},{391,7},{3... | collective-permute-start | bytes 3080 | tf_op jit(solution)/shard_map/ppermute | solution.py:10
  24.1 7.6 %collective-permute-start.4 = (bf16[512]{0:T(512)(128)(2,1)S(1)}, bf16[512]{0:T(512)(128)(2,1)S(1)}, u32[]{:S(2)}, u32[]{:S(2)}) collective-permute-start(bf16[512]{0:T(512)(128)(2,1)S(1)} %fusion.6), channel_id=1, source_target_pairs={{1,0},{2,1},{3,2},{4,3},{5,4},{6,5},{7,6},{8,7},{9,8},{10,9},{11,1... | collective-permute-start | bytes 3080 | tf_op jit(solution)/shard_map/ppermute | solution.py:10
  31.7 3.5 %constant_dynamic-update-slice_fusion.2 = (bf16[512,2560]{0,1:T(8,128)(2,1)S(1)}, bf16[512,512]{0,1:T(8,128)(2,1)S(1)}) fusion(bf16[512,2048]{1,0:T(8,128)(2,1)} %param.2), kind=kOutput, calls=%fused_computation.12 | convolution fusion | flops 1074003968 | bytes 5242880 | tf_op jit(solution)/shard_map/dot_general | solution.py:14
  35.2 0.0 collective-permute-done.5
  35.2 1.9 collective-permute-start.6
  37.2 0.0 copy-done.4
  37.2 0.2 fusion.4
  37.3 0.0 collective-permute-done.7
  37.4 0.7 collective-permute-done.4
  38.0 18.9 %collective-permute-done.6 = bf16[512]{0:T(512)(128)(2,1)S(1)} collective-permute-done((bf16[512]{0:T(512)(128)(2,1)S(1)}, bf16[512]{0:T(512)(128)(2,1)S(1)}, u32[]{:S(2)}, u32[]{:S(2)}) %collective-permute-start.6) | collective-permute-done | bytes 1056 | tf_op jit(solution)/shard_map/ppermute | solution.py:10
  56.9 0.0 collective-permute-done
  56.9 0.0 copy-done.5
  56.9 2.1 convolution_convert_fusion.1
  59.0 1.9 collective-permute-start.1
  60.9 2.0 copy.7
  63.0 0.0 copy-start.3
  63.0 0.0 collective-permute-done.2
  63.0 3.6 %convolution_convert_fusion = bf16[512,512]{1,0:T(8,128)(2,1)S(1)} fusion(bf16[512,2048]{1,0:T(8,128)(2,1)} %param.2, bf16[512,2048]{1,0:T(8,128)(2,1)} %collective-permute-done.2), kind=kOutput, calls=%fused_computation | convolution fusion | flops 1074003968 | bytes 4718592 | tf_op jit(solution)/shard_map/dot_general | solution.py:14
  66.6 0.0 copy-start.2
  66.6 3.6 %collective-permute-start.3 = (bf16[512,512]{1,0:T(8,128)(2,1)S(1)}, bf16[512,512]{1,0:T(8,128)(2,1)S(1)}, u32[]{:S(2)}, u32[]{:S(2)}) collective-permute-start(bf16[512,512]{1,0:T(8,128)(2,1)S(1)} %convolution_convert_fusion), channel_id=1, source_target_pairs={{384,0},{385,1},{386,2},{387,3},{388,4},{389,5},{390,6},{391,7},{3... | collective-permute-start | bytes 1572872 | tf_op jit(solution)/shard_map/ppermute | solution.py:10
  70.2 1.3 fusion.9
  71.5 0.0 copy-done.3
  71.5 0.1 constant_dynamic-update-slice_fusion.1
  71.6 0.2 fusion.10
  71.8 25.2 %collective-permute-done.1 = bf16[512,512]{1,0:T(8,128)(2,1)S(1)} collective-permute-done((bf16[512,512]{1,0:T(8,128)(2,1)}, bf16[512,512]{1,0:T(8,128)(2,1)S(1)}, u32[]{:S(2)}, u32[]{:S(2)}) %collective-permute-start.1) | collective-permute-done | bytes 524320 | tf_op jit(solution)/shard_map/ppermute | solution.py:10
  97.0 0.2 fusion.2
  97.2 0.0 collective-permute-done.3
  97.2 0.8 copy-done
  98.0 0.2 fusion
  98.2 0.0 copy-done.2
  98.2 0.1 convolution_bitcast_fusion
  98.3 2.1 copy.8
  100.4 106.3 %psum.14 = f32[8]{0:T(128)S(1)} all-reduce(f32[8]{0:T(128)S(1)} %convolution_bitcast_fusion), channel_id=1, replica_groups=mesh['dp'=512] {'dp'}, use_global_device_ids=true, to_apply=%region_0.0 | all-reduce | flops 8 | bytes 64 | tf_op jit(solution)/shard_map/psum | solution.py:39
  206.6 0.1 fusion.7
  206.8 0.6 multiply_reduce_fusion
  207.4 94.7 %psum.15 = f32[]{:T(128)} all-reduce(f32[]{:T(128)} %get-tuple-element.6), channel_id=1, replica_groups=mesh['dp'=512] {'dp'}, use_global_device_ids=true, to_apply=%region_2.0 | all-reduce | flops 1 | bytes 8 | tf_op jit(solution)/shard_map/psum | solution.py:41
  302.8 0.0 copy-start.1
  302.8 1.1 constant_dynamic-update-slice_fusion
  304.0 0.0 copy-done.1
  304.0 2.8 copy.9
  306.8 0.6 broadcast_divide_fusion
  307.4 0.6 pad_maximum_fusion
  (9 shorter events, 0.1 us)
Async XLA Ops:
  0.6 56.3 %collective-permute-start = (bf16[512,2048]{1,0:T(8,128)(2,1)}, bf16[512,2048]{1,0:T(8,128)(2,1)S(1)}, u32[]{:S(2)}, u32[]{:S(2)}) collective-permute-start(bf16[512,2048]{1,0:T(8,128)(2,1)} %param.2), channel_id=1, source_target_pairs={{1,0},{2,1},{3,2},{4,3},{5,4},{6,5},{7,6},{8,7},{9,8},{10,9},{11,1... | collective-permute-start | bytes 6291464 | tf_op jit(solution)/shard_map/ppermute | solution.py:10
  14.2 48.8 %collective-permute-start.2 = (bf16[512,2048]{1,0:T(8,128)(2,1)}, bf16[512,2048]{1,0:T(8,128)(2,1)}, u32[]{:S(2)}, u32[]{:S(2)}) collective-permute-start(bf16[512,2048]{1,0:T(8,128)(2,1)} %param.2), channel_id=1, source_target_pairs={{128,0},{129,1},{130,2},{131,3},{132,4},{133,5},{134,6},{135,7},{1... | collective-permute-start | bytes 6291464 | tf_op jit(solution)/shard_map/ppermute | solution.py:10
  17.4 19.8 %copy-start.4 = (f32[8,512]{1,0:T(8,128)S(1)}, f32[8,512]{1,0:T(8,128)}, u32[]{:S(2)}) copy-start(f32[8,512]{1,0:T(8,128)} %param.3) | copy-start | bytes 49156
  17.4 39.5 %copy-start.5 = (bf16[512,2048]{1,0:T(8,128)(2,1)S(1)}, bf16[512,2048]{1,0:T(8,128)(2,1)}, u32[]{:S(2)}) copy-start(bf16[512,2048]{1,0:T(8,128)(2,1)} %param.2) | copy-start | bytes 6291460
  17.4 17.8 %collective-permute-start.5 = (bf16[512]{0:T(512)(128)(2,1)S(1)}, bf16[512]{0:T(512)(128)(2,1)S(1)}, u32[]{:S(2)}, u32[]{:S(2)}) collective-permute-start(bf16[512]{0:T(512)(128)(2,1)S(1)} %fusion.6), channel_id=1, source_target_pairs={{511,0},{0,1},{1,2},{2,3},{3,4},{4,5},{5,6},{6,7},{7,8},{8,9},{9,1... | collective-permute-start | bytes 3080 | tf_op jit(solution)/shard_map/ppermute | solution.py:10
  19.5 17.9 %collective-permute-start.7 = (bf16[512]{0:T(512)(128)(2,1)S(1)}, bf16[512]{0:T(512)(128)(2,1)S(1)}, u32[]{:S(2)}, u32[]{:S(2)}) collective-permute-start(bf16[512]{0:T(512)(128)(2,1)S(1)} %fusion.6), channel_id=1, source_target_pairs={{384,0},{385,1},{386,2},{387,3},{388,4},{389,5},{390,6},{391,7},{3... | collective-permute-start | bytes 3080 | tf_op jit(solution)/shard_map/ppermute | solution.py:10
  24.1 14.0 %collective-permute-start.4 = (bf16[512]{0:T(512)(128)(2,1)S(1)}, bf16[512]{0:T(512)(128)(2,1)S(1)}, u32[]{:S(2)}, u32[]{:S(2)}) collective-permute-start(bf16[512]{0:T(512)(128)(2,1)S(1)} %fusion.6), channel_id=1, source_target_pairs={{1,0},{2,1},{3,2},{4,3},{5,4},{6,5},{7,6},{8,7},{9,8},{10,9},{11,1... | collective-permute-start | bytes 3080 | tf_op jit(solution)/shard_map/ppermute | solution.py:10
  35.2 21.7 %collective-permute-start.6 = (bf16[512]{0:T(512)(128)(2,1)S(1)}, bf16[512]{0:T(512)(128)(2,1)S(1)}, u32[]{:S(2)}, u32[]{:S(2)}) collective-permute-start(bf16[512]{0:T(512)(128)(2,1)S(1)} %fusion.6), channel_id=1, source_target_pairs={{128,0},{129,1},{130,2},{131,3},{132,4},{133,5},{134,6},{135,7},{1... | collective-permute-start | bytes 3080 | tf_op jit(solution)/shard_map/ppermute | solution.py:10
  59.0 38.0 %collective-permute-start.1 = (bf16[512,512]{1,0:T(8,128)(2,1)}, bf16[512,512]{1,0:T(8,128)(2,1)S(1)}, u32[]{:S(2)}, u32[]{:S(2)}) collective-permute-start(bf16[512,512]{1,0:T(8,128)(2,1)} %convolution_convert_fusion.1), channel_id=1, source_target_pairs={{511,0},{0,1},{1,2},{2,3},{3,4},{4,5},{5,6},{6,7},{7,8},{8,9},{9,1... | collective-permute-start | bytes 1572872 | tf_op jit(solution)/shard_map/ppermute | solution.py:10
  63.0 8.5 %copy-start.3 = (bf16[512,512]{0,1:T(8,128)(2,1)S(1)}, bf16[512,512]{0,1:T(8,128)(2,1)}, u32[]{:S(2)}) copy-start(bf16[512,512]{0,1:T(8,128)(2,1)} %copy.7) | copy-start | bytes 1572868
  66.6 31.6 %copy-start.2 = (bf16[512,512]{1,0:T(8,128)(2,1)}, bf16[512,512]{1,0:T(8,128)(2,1)S(1)}, u32[]{:S(2)}) copy-start(bf16[512,512]{1,0:T(8,128)(2,1)S(1)} %convolution_convert_fusion) | copy-start | bytes 1572868
  66.6 30.6 %collective-permute-start.3 = (bf16[512,512]{1,0:T(8,128)(2,1)S(1)}, bf16[512,512]{1,0:T(8,128)(2,1)S(1)}, u32[]{:S(2)}, u32[]{:S(2)}) collective-permute-start(bf16[512,512]{1,0:T(8,128)(2,1)S(1)} %convolution_convert_fusion), channel_id=1, source_target_pairs={{384,0},{385,1},{386,2},{387,3},{388,4},{389,5},{390,6},{391,7},{3... | collective-permute-start | bytes 1572872 | tf_op jit(solution)/shard_map/ppermute | solution.py:10
  97.2 0.8 copy-start
  302.8 1.2 copy-start.1
where the time goes:
time: 310 us; the launch traced here: 308 us
  blocking collectives  201 us (65%)
  waiting for transfers between devices  44.8 us (14%)
  starting transfers between devices  37.7 us (12%)
  matrix products  11.4 us (4%)
  local copies, waits for them, and re-layouts  9.75 us (3%)
    psum x1, blocking collectives, on_device(): coeffs = lax.psum(partial_value, 'dp') / total_rows  106 us
    psum x1, blocking collectives, on_device(): square_sum = lax.psum(jnp.sum(remainder * remainder), 'dp')  94.7 us
    ppermute x8, waiting for transfers between devices, shifted(): return lax.ppermute(block, axis, route)  44.8 us
    ppermute x8, starting transfers between devices, shifted(): return lax.ppermute(block, axis, route)  37.7 us
    dot_general x3, matrix products, pair_block(): lax.dot_general(left_rows, right_rows, (((1,), (1,)), ((), ())), preferre...  9.16 us
  transfers between devices with their start and end apart: 8, of which 3 were waited for; matrix products, arithmetic and copies ran while one was open for 5% of the time, Pallas kernels for 0%

commit v1 on v0

v1 whole, which is shorter than its diff:
```python
import functools

import jax
import jax.numpy as jnp
import numpy as np
from jax import lax
from jax.experimental import pallas as pl
from jax.experimental.pallas import tpu as pltpu
from jax.sharding import Mesh
from jax.sharding import PartitionSpec as P

AXES = ("x", "z", "y", "core")
SIZES = (4, 8, 8, 2)
FIRST_GROUP = ("z", "core")
SECOND_GROUP = ("x", "y")
BANDS = 5
VMEM_BYTES = 40 * 1024 * 1024
F32 = jnp.float32
BF16 = jnp.bfloat16


def dot_last(left, right, precision=None):
    return lax.dot_general(
        left, right, (((1,), (1,)), ((), ())), preferred_element_type=F32, precision=precision
    )


def params(**more):
    return pltpu.CompilerParams(vmem_limit_bytes=VMEM_BYTES, **more)


def whole(memory_space=pltpu.VMEM):
    return pl.BlockSpec(memory_space=memory_space)


def sketch_image_kernel(sketch_ref, basis_ref, u_ref):
    last = basis_ref.shape[0] - 1
    current = basis_ref[last : last + 1, :].astype(BF16)
    rows = jnp.broadcast_to(current, (16, current.shape[1]))
    product = jnp.dot(rows, sketch_ref[...], preferred_element_type=F32)
    u_ref[...] = product[0:1, :]


def sketch_image(sketch, basis):
    return pl.pallas_call(
        sketch_image_kernel,
        out_shape=jax.ShapeDtypeStruct((1, sketch.shape[1]), F32),
        in_specs=[whole(), whole()],
        out_specs=whole(),
        compiler_params=params(),
        cost_estimate=pl.CostEstimate(flops=2 * sketch.size, bytes_accessed=2 * sketch.size, transcendentals=0),
    )(sketch, basis)


def own_block_kernel(sketch_ref, basis_ref, rows_ref, own_image_ref):
    last = basis_ref.shape[0] - 1
    current = basis_ref[last : last + 1, :].astype(BF16)
    block = dot_last(sketch_ref[...], sketch_ref[...]).astype(BF16)
    rows_ref[...] = block
    vec = jnp.broadcast_to(current, (16, current.shape[1]))
    own_image_ref[...] = dot_last(vec, block)[0:1, :]


def own_block(sketch, basis):
    n, k = sketch.shape
    return pl.pallas_call(
        own_block_kernel,
        grid=(1,),
        out_shape=(
            jax.ShapeDtypeStruct((n, BANDS * n), BF16),
            jax.ShapeDtypeStruct((1, n), F32),
        ),
        in_specs=[
            pl.BlockSpec((n, k), lambda i: (0, 0)),
            pl.BlockSpec(basis.shape, lambda i: (0, 0)),
        ],
        out_specs=(
            pl.BlockSpec((n, n), lambda i: (0, 0)),
            pl.BlockSpec((1, n), lambda i: (0, 0)),
        ),
        compiler_params=params(),
        cost_estimate=pl.CostEstimate(flops=2 * n * n * k, bytes_accessed=2 * n * k, transcendentals=0),
    )(sketch, basis)


def image_kernel(sketch_ref, basis_ref, own_ref, a_ref, b_ref, c_ref, d_ref, image_ref, sums_ref):
    total = (a_ref[...] + b_ref[...]) + (c_ref[...] + d_ref[...])
    high = total.astype(BF16).astype(F32)
    rest = total - high
    middle = rest.astype(BF16).astype(F32)
    low = rest - middle
    row = lax.broadcasted_iota(jnp.int32, (16, total.shape[1]), 0)
    parts = jnp.where(row == 0, high, jnp.where(row == 1, middle, jnp.where(row == 2, low, 0.0)))
    product = dot_last(parts.astype(BF16), sketch_ref[...])
    image = (product[2:3, :] + product[1:2, :]) + product[0:1, :] + own_ref[...]
    image_ref[...] = image
    basis = basis_ref[...]
    m, n = basis.shape
    place = lax.broadcasted_iota(jnp.int32, (128 - m, n), 0)
    right = jnp.concatenate([basis, jnp.where(place == 0, image, 0.0)], axis=0)
    products = dot_last(basis, right, precision=lax.Precision.HIGHEST)
    norm = jnp.sum(image * image)
    lane = lax.broadcasted_iota(jnp.int32, products.shape, 1)
    sums_ref[...] = jnp.where(lane == m + 1, norm, products)


def image_and_sums(sketch, basis, own_image, parts):
    n, k = sketch.shape
    return pl.pallas_call(
        image_kernel,
        out_shape=(
            jax.ShapeDtypeStruct((1, n), F32),
            jax.ShapeDtypeStruct((basis.shape[0], 128), F32),
        ),
        in_specs=[whole()] * 7,
        out_specs=(whole(), whole()),
        compiler_params=params(),
        cost_estimate=pl.CostEstimate(flops=2 * n * k * 16, bytes_accessed=2 * n * k, transcendentals=0),
    )(sketch, basis, own_image, *parts)


def pair_kernel(column_ref, sketch_ref, other_ref, rows_in_ref, rows_ref, back_ref):
    del column_ref, rows_in_ref
    rows_ref[...] = dot_last(sketch_ref[...], other_ref[...]).astype(BF16)
    back_ref[...] = dot_last(other_ref[...], sketch_ref[...]).astype(BF16)


def pair_blocks(column, sketch, other, rows):
    n, k = sketch.shape
    return pl.pallas_call(
        pair_kernel,
        grid_spec=pltpu.PrefetchScalarGridSpec(
            num_scalar_prefetch=1,
            grid=(1,),
            in_specs=[
                pl.BlockSpec((n, k), lambda i, c: (0, 0)),
                pl.BlockSpec((n, k), lambda i, c: (0, 0)),
                pl.BlockSpec(memory_space=pl.ANY),
            ],
            out_specs=(
                pl.BlockSpec((n, n), lambda i, c: (0, c[0])),
                pl.BlockSpec((n, n), lambda i, c: (0, 0)),
            ),
        ),
        out_shape=(
            jax.ShapeDtypeStruct(rows.shape, rows.dtype),
            jax.ShapeDtypeStruct((n, n), BF16),
        ),
        input_output_aliases={3: 0},
        compiler_params=params(),
        cost_estimate=pl.CostEstimate(flops=4 * n * n * k, bytes_accessed=4 * n * k, transcendentals=0),
    )(column, sketch, other, rows)


def place_kernel(column_ref, block_ref, rows_in_ref, rows_ref):
    del column_ref, rows_in_ref
    rows_ref[...] = block_ref[...]


def place_block(column, block, rows):
    n = block.shape[0]
    return pl.pallas_call(
        place_kernel,
        grid_spec=pltpu.PrefetchScalarGridSpec(
            num_scalar_prefetch=1,
            grid=(1,),
            in_specs=[
                pl.BlockSpec((n, n), lambda i, c: (0, 0)),
                pl.BlockSpec(memory_space=pl.ANY),
            ],
            out_specs=pl.BlockSpec((n, n), lambda i, c: (0, c[0])),
        ),
        out_shape=jax.ShapeDtypeStruct(rows.shape, rows.dtype),
        input_output_aliases={2: 0},
        compiler_params=params(),
        cost_estimate=pl.CostEstimate(flops=0, bytes_accessed=4 * n * n, transcendentals=0),
    )(column, block, rows)


def finish_kernel(count, sums_ref, basis_ref, image_ref, left_ref, stats_ref):
    sums = jnp.sum(sums_ref[...], axis=0)
    basis = basis_ref[...]
    m = basis.shape[0]
    row = lax.broadcasted_iota(jnp.int32, sums.shape, 0)
    lane = lax.broadcasted_iota(jnp.int32, sums.shape, 1)
    inner = jnp.sum(jnp.where(lane == m, sums, 0.0), axis=1, keepdims=True)
    norm = jnp.sum(jnp.where((lane == m + 1) & (row == 0), sums, 0.0))
    coeffs = inner / count
    across = jnp.sum(jnp.where(lane == row, coeffs, 0.0), axis=0, keepdims=True)
    gram = jnp.where(lane < m, sums, 0.0)
    quadratic = jnp.sum(jnp.sum(coeffs * gram, axis=0, keepdims=True) * across)
    cross = jnp.sum(coeffs * inner)
    square = (norm - cross) + (quadratic - cross)
    left_ref[...] = image_ref[...] - jnp.sum(coeffs * basis, axis=0, keepdims=True)
    lane_row = lax.broadcasted_iota(jnp.int32, across.shape, 1)
    stats = jnp.where(lane_row == m, square, across)
    stats_ref[...] = jnp.where(lane_row == m + 1, norm, stats)


def finish(sums, basis, image, count):
    n = image.shape[1]
    return pl.pallas_call(
        functools.partial(finish_kernel, count),
        out_shape=(
            jax.ShapeDtypeStruct((1, n), F32),
            jax.ShapeDtypeStruct((1, 128), F32),
        ),
        in_specs=[whole()] * 3,
        out_specs=(whole(), whole()),
        compiler_params=params(),
    )(sums, basis, image)


def everyones(block, group):
    members = 1
    for name in group:
        members *= lax.axis_size(name)
    copies = jnp.broadcast_to(block[None], (members, *block.shape))
    return lax.all_to_all(copies, group, 0, 0, tiled=True)


def on_device(sketch, basis):
    devices = 1
    for name in AXES:
        devices *= lax.axis_size(name)
    stride = devices // 4
    total_rows = sketch.shape[0] * devices
    is_second = lax.axis_index("core")

    def move(block, source_of):
        return lax.ppermute(block, AXES, [(source_of(i) % devices, i) for i in range(devices)])

    u = sketch_image(sketch, basis)
    parts = [
        move(u, lambda i: i ^ 1),
        move(u, lambda i: i - 1 if i % 2 == 0 else i + 1),
        move(u, lambda i: i + stride),
        move(u, lambda i: i - stride),
    ]
    far = move(sketch, lambda i: i + stride if i % 2 == 0 else i - stride)
    near = move(sketch, lambda i: i + 1)
    rows, own_image = own_block(sketch, basis)
    image, sums = image_and_sums(sketch, basis, own_image, parts)
    sums = jnp.sum(everyones(sums, FIRST_GROUP), axis=0)
    sums = everyones(sums, SECOND_GROUP)

    one = jnp.ones((1,), jnp.int32)
    far_column = (3 + is_second).astype(jnp.int32)[None]
    rows, far_back = pair_blocks(far_column, sketch, far, rows)
    far_back = move(far_back, lambda i: i - stride if i % 2 == 0 else i + stride)
    rows, near_back = pair_blocks(one, sketch, near, rows)
    near_back = move(near_back, lambda i: i - 1)

    left, stats = finish(sums, basis, image, float(total_rows))
    m = basis.shape[0]
    square, norm = stats[0, m], stats[0, m + 1]
    square = lax.cond(
        square < 1e-3 * norm,
        lambda: lax.psum(jnp.sum(left * left), AXES),
        lambda: square,
    )
    beta = jnp.sqrt(square / total_rows + 1e-06)
    next_vector = left[0] / beta
    coefficients = jnp.concatenate([stats[0, :m], beta[None]])

    rows = place_block(7 - far_column, far_back, rows)
    rows = place_block(2 * one, near_back, rows)
    return rows, next_vector, coefficients


def solution(mesh):
    grid = Mesh(np.asarray(mesh.devices).reshape(SIZES), AXES)
    return jax.shard_map(
        on_device,
        mesh=grid,
        in_specs=(P(AXES, None), P(None, AXES)),
        out_specs=(P(AXES, None), P(AXES), P()),
        check_vma=False,
    )
```

time: 310 us -> 120 us (0.39)
  blocking collectives: 201 us -> 10.4 us
  starting transfers between devices: 37.7 us -> 61.9 us
  waiting for transfers between devices: 44.8 us -> 26.3 us
  Pallas kernels: 0 us -> 13.1 us
  matrix products: 11.4 us -> 0 us
  local copies, waits for them, and re-layouts: 9.75 us -> 3.66 us
    psum x2 -> x0, blocking collectives: 201 us -> none  [the longest x1 106 us: on_device(): coeffs = lax.psum(partial_value, 'dp') / total_rows]
    ppermute x8, waiting for transfers between devices: 44.8 us -> 17.3 us  [move(): lax.ppermute(block, AXES, [(source_of(i) % devices, i) for i in range(dev...]
    all_to_all x0 -> x1, starting transfers between devices: none -> 27.2 us  [everyones(): return lax.all_to_all(copies, group, 0, 0, tiled=True)]
    pallas_call x0 -> x8, Pallas kernels: none -> 13.1 us  [the longest x2 7.91 us: pair_blocks(): pl.pallas_call(pair_kernel, grid_spec=pltpu.PrefetchScalarGridSpec(num_sc...]
    dot_general x10 -> x0, matrix products: 11.4 us -> none  [the longest x3 9.16 us: pair_block(): lax.dot_general(left_rows, right_rows, (((1,), (1,)), ((), ())), preferre...]
    all_to_all x0 -> x1, blocking collectives: none -> 10.4 us  [everyones(): return lax.all_to_all(copies, group, 0, 0, tiled=True)]
    all_to_all x0 -> x1, waiting for transfers between devices: none -> 8.92 us  [everyones(): return lax.all_to_all(copies, group, 0, 0, tiled=True)]
    convert_element_type x2 -> x0, local copies, waits for them, and re-layouts: 4.12 us -> none  [pair_block(): return lax.dot_general(left_rows, right_rows, (((1,), (1,)), ((), ())), p...]
  transfers between devices with their start and end apart: 8 -> 9, of which waited for: 3 -> 3; matrix products, arithmetic and copies ran while one was open for 5% -> 2% of each run, Pallas kernels for 0% -> 10%
where the time goes in v1:
time: 120 us; the launch traced here: 119 us
  starting transfers between devices  61.9 us (52%)
  waiting for transfers between devices  26.3 us (22%)
  Pallas kernels  13.1 us (11%)
  blocking collectives  10.4 us (9%)
  local copies, waits for them, and re-layouts  3.66 us (3%)
  between operations  2.14 us (2%)
    ppermute x8, starting transfers between devices, move(): lax.ppermute(block, AXES, [(source_of(i) % devices, i) for i in range(dev...  34.8 us
    all_to_all x1, starting transfers between devices, everyones(): return lax.all_to_all(copies, group, 0, 0, tiled=True)  27.2 us
    ppermute x8, waiting for transfers between devices, move(): lax.ppermute(block, AXES, [(source_of(i) % devices, i) for i in range(dev...  17.3 us
    all_to_all x1, blocking collectives, everyones(): return lax.all_to_all(copies, group, 0, 0, tiled=True)  10.4 us
    all_to_all x1, waiting for transfers between devices, everyones(): return lax.all_to_all(copies, group, 0, 0, tiled=True)  8.92 us
    pallas_call x2, Pallas kernels, pair_blocks(): pl.pallas_call(pair_kernel, grid_spec=pltpu.PrefetchScalarGridSpec(num_sc...  7.91 us
  transfers between devices with their start and end apart: 9, of which 3 were waited for; matrix products, arithmetic and copies ran while one was open for 2% of the time, Pallas kernels for 10%

profile of v1, /device:TPU:6, one launch (start us, length us, event | category | flops | bytes accessed | tf_op | source)
XLA Modules:
  0.0 119.4 jit_solution(14027523030599208542)
XLA Ops:
  0.6 2.7 %collective-permute-start.1 = (bf16[512,2048]{1,0:T(8,128)(2,1)}, bf16[512,2048]{1,0:T(8,128)(2,1)}, u32[]{:S(2)}, u32[]{:S(2)}) collective-permute-start(bf16[512,2048]{1,0:T(8,128)(2,1)} %sketch_ref.9), channel_id=1, source_target_pairs={{128,0},{385,1},{130,2},{387,3},{132,4},{389,5},{134,6},{391,7},{1... | collective-permute-start | bytes 6291464 | tf_op jit(solution)/shard_map/ppermute | solution.py:231
  3.4 13.7 %collective-permute-start = (bf16[512,2048]{1,0:T(8,128)(2,1)}, bf16[512,2048]{1,0:T(8,128)(2,1)}, u32[]{:S(2)}, u32[]{:S(2)}) collective-permute-start(bf16[512,2048]{1,0:T(8,128)(2,1)} %sketch_ref.9), channel_id=1, source_target_pairs={{1,0},{2,1},{3,2},{4,3},{5,4},{6,5},{7,6},{8,7},{9,8},{10,9},{11,1... | collective-permute-start | bytes 6291464 | tf_op jit(solution)/shard_map/ppermute | solution.py:231
  17.0 0.0 copy-start
  17.0 1.6 %copy-done = bf16[512,2048]{1,0:T(8,128)(2,1)S(1)} copy-done((bf16[512,2048]{1,0:T(8,128)(2,1)S(1)}, bf16[512,2048]{1,0:T(8,128)(2,1)}, u32[]{:S(2)}) %copy-start) | copy-done | bytes 2097176
  18.6 0.0 copy-start.2
  18.6 0.7 copy-done.2
  19.4 0.4 shard_map.54
  19.7 0.0 copy-start.3
  19.7 0.0 copy-start.1
  19.7 2.1 %collective-permute-start.4 = (f32[1,2048]{1,0:T(1,128)S(1)}, f32[1,2048]{1,0:T(1,128)S(1)}, u32[]{:S(2)}, u32[]{:S(2)}) collective-permute-start(f32[1,2048]{1,0:T(1,128)S(1)} %shard_map.54), channel_id=1, source_target_pairs={{1,0},{0,1},{3,2},{2,3},{5,4},{4,5},{7,6},{6,7},{9,8},{8,9},{11,10... | collective-permute-start | bytes 24584 | tf_op jit(solution)/shard_map/ppermute | solution.py:231
  21.8 3.4 %collective-permute-start.5 = (f32[1,2048]{1,0:T(1,128)S(1)}, f32[1,2048]{1,0:T(1,128)S(1)}, u32[]{:S(2)}, u32[]{:S(2)}) collective-permute-start(f32[1,2048]{1,0:T(1,128)S(1)} %shard_map.54), channel_id=1, source_target_pairs={{511,0},{2,1},{1,2},{4,3},{3,4},{6,5},{5,6},{8,7},{7,8},{10,9},{9,... | collective-permute-start | bytes 24584 | tf_op jit(solution)/shard_map/ppermute | solution.py:231
  25.2 2.7 %collective-permute-start.6 = (f32[1,2048]{1,0:T(1,128)S(1)}, f32[1,2048]{1,0:T(1,128)S(1)}, u32[]{:S(2)}, u32[]{:S(2)}) collective-permute-start(f32[1,2048]{1,0:T(1,128)S(1)} %shard_map.54), channel_id=1, source_target_pairs={{128,0},{129,1},{130,2},{131,3},{132,4},{133,5},{134,6},{135,7},{1... | collective-permute-start | bytes 24584 | tf_op jit(solution)/shard_map/ppermute | solution.py:231
  27.9 0.0 collective-permute-done.4.a_ref
  27.9 4.3 %collective-permute-start.7 = (f32[1,2048]{1,0:T(1,128)S(1)}, f32[1,2048]{1,0:T(1,128)S(1)}, u32[]{:S(2)}, u32[]{:S(2)}) collective-permute-start(f32[1,2048]{1,0:T(1,128)S(1)} %shard_map.54), channel_id=1, source_target_pairs={{384,0},{385,1},{386,2},{387,3},{388,4},{389,5},{390,6},{391,7},{3... | collective-permute-start | bytes 24584 | tf_op jit(solution)/shard_map/ppermute | solution.py:231
  32.2 2.1 %shard_map.49 = (bf16[512,2560]{1,0:T(8,128)(2,1)}, f32[1,512]{1,0:T(1,128)S(1)}) custom-call(bf16[512,2048]{1,0:T(8,128)(2,1)S(1)} %copy-done, f32[8,512]{1,0:T(8,128)S(1)} %copy-done.2), custom_call_target="tpu_custom_call" | custom-call | flops 1073741824 | bytes 2097152 | tf_op jit(solution)/shard_map/pallas_call | solution.py:66
  34.3 6.6 %collective-permute-done.5.b_ref = f32[1,2048]{1,0:T(1,128)S(1)} collective-permute-done((f32[1,2048]{1,0:T(1,128)S(1)}, f32[1,2048]{1,0:T(1,128)S(1)}, u32[]{:S(2)}, u32[]{:S(2)}) %collective-permute-start.5) | collective-permute-done | bytes 8224 | tf_op jit(solution)/shard_map/ppermute | solution.py:231
  40.9 0.0 collective-permute-done.6.c_ref
  40.9 0.0 collective-permute-done.7.d_ref
  40.9 0.8 shard_map.55
  41.7 10.4 %all_to_all.10 = f32[16,8,128]{2,1,0:T(8,128)S(1)} all-to-all(f32[16,8,128]{2,1,0:T(8,128)S(1)} %broadcast_in_dim.25), channel_id=1, replica_groups=mesh['x'=4,'z'=8,'y'=8,'core'=2] {'z','core'}, dimensions={0} | all-to-all | bytes 131072 | tf_op jit(solution)/shard_map/all_to_all | solution.py:219
  52.1 0.7 broadcast_in_dim.26
  52.8 27.2 %all-to-all-start.1 = ((f32[32,8,128]{2,1,0:T(8,128)}), f32[32,8,128]{2,1,0:T(8,128)S(1)}, u32[]{:S(2)}, u32[]{:S(2)}) async-start(f32[32,8,128]{2,1,0:T(8,128)} %broadcast_in_dim.26), calls=%async_computation.1 | async-start | bytes 262144 | tf_op jit(solution)/shard_map/all_to_all | solution.py:219
  80.0 8.9 %all-to-all-done.1.sums_ref = f32[32,8,128]{2,1,0:T(8,128)S(1)} async-done(((f32[32,8,128]{2,1,0:T(8,128)}), f32[32,8,128]{2,1,0:T(8,128)S(1)}, u32[]{:S(2)}, u32[]{:S(2)}) %all-to-all-start.1) | async-done | bytes 131104 | tf_op jit(solution)/shard_map/all_to_all | solution.py:219
  88.9 0.0 copy-done.3
  88.9 0.2 shard_map.56
  89.1 0.7 fusion
  91.1 0.7 conditional.1
  91.9 0.0 collective-permute-done.1.other_ref
  91.9 0.0 copy-done.1
  91.9 4.0 %shard_map.50 = (bf16[512,2560]{1,0:T(8,128)(2,1)}, bf16[512,512]{1,0:T(8,128)(2,1)S(1)}) custom-call(s32[1]{0:T(128)} %bitcast.column_ref, bf16[512,2048]{1,0:T(8,128)(2,1)S(1)} %copy-done.1, bf16[512,2048]{1,0:T(8,128)(2,1)} %collective-permute-done.1.other_ref, bf16[512,2560]{1,0:T(8,128)(2,1)} %get-tuple-element.25.rows_in_ref), custom_call_target="tpu_custom_call", output_to_operand_aliasing={{0}: (3, {})} | custom-call | flops 2147483648 | bytes 4194304 | tf_op jit(solution)/shard_map/pallas_call | solution.py:130
  95.9 4.0 %collective-permute-start.3 = (bf16[512,512]{1,0:T(8,128)(2,1)S(1)}, bf16[512,512]{1,0:T(8,128)(2,1)S(1)}, u32[]{:S(2)}, u32[]{:S(2)}) collective-permute-start(bf16[512,512]{1,0:T(8,128)(2,1)S(1)} %get-tuple-element.28), channel_id=1, source_target_pairs={{384,0},{129,1},{386,2},{131,3},{388,4},{133,5},{390,6},{135,7},{3... | collective-permute-start | bytes 1572872 | tf_op jit(solution)/shard_map/ppermute | solution.py:231
  99.9 0.0 collective-permute-done.other_ref
  99.9 4.0 %shard_map.51 = (bf16[512,2560]{1,0:T(8,128)(2,1)}, bf16[512,512]{1,0:T(8,128)(2,1)S(1)}) custom-call(s32[1]{0:T(128)} %constant.7.clone.1.column_ref, bf16[512,2048]{1,0:T(8,128)(2,1)S(1)} %copy-done.1, bf16[512,2048]{1,0:T(8,128)(2,1)} %collective-permute-done.other_ref, ...), custom_call_target="tpu_custom_call", output_to_operand_aliasing={{0}: (3, {})} | custom-call | flops 2147483648 | bytes 4194304 | tf_op jit(solution)/shard_map/pallas_call | solution.py:130
  103.8 1.9 %collective-permute-start.2 = (bf16[512,512]{1,0:T(8,128)(2,1)S(1)}, bf16[512,512]{1,0:T(8,128)(2,1)S(1)}, u32[]{:S(2)}, u32[]{:S(2)}) collective-permute-start(bf16[512,512]{1,0:T(8,128)(2,1)S(1)} %get-tuple-element.27), channel_id=1, source_target_pairs={{511,0},{0,1},{1,2},{2,3},{3,4},{4,5},{5,6},{6,7},{7,8},{8,9},{9,1... | collective-permute-start | bytes 1572872 | tf_op jit(solution)/shard_map/ppermute | solution.py:231
  105.8 0.6 pad_maximum_fusion
  106.4 0.6 broadcast_divide_fusion
  106.9 0.0 collective-permute-done.3.block_ref
  106.9 0.8 shard_map.52.rows_in_ref
  107.8 10.8 %collective-permute-done.2.block_ref = bf16[512,512]{1,0:T(8,128)(2,1)S(1)} collective-permute-done((bf16[512,512]{1,0:T(8,128)(2,1)S(1)}, bf16[512,512]{1,0:T(8,128)(2,1)S(1)}, u32[]{:S(2)}, u32[]{:S(2)}) %collective-permute-start.2) | collective-permute-done | bytes 524320 | tf_op jit(solution)/shard_map/ppermute | solution.py:231
  118.6 0.8 shard_map.53
  (3 shorter events, 0.0 us)
Async XLA Ops:
  0.6 91.3 %collective-permute-start.1 = (bf16[512,2048]{1,0:T(8,128)(2,1)}, bf16[512,2048]{1,0:T(8,128)(2,1)}, u32[]{:S(2)}, u32[]{:S(2)}) collective-permute-start(bf16[512,2048]{1,0:T(8,128)(2,1)} %sketch_ref.9), channel_id=1, source_target_pairs={{128,0},{385,1},{130,2},{387,3},{132,4},{389,5},{134,6},{391,7},{1... | collective-permute-start | bytes 6291464 | tf_op jit(solution)/shard_map/ppermute | solution.py:231
  3.4 96.5 %collective-permute-start = (bf16[512,2048]{1,0:T(8,128)(2,1)}, bf16[512,2048]{1,0:T(8,128)(2,1)}, u32[]{:S(2)}, u32[]{:S(2)}) collective-permute-start(bf16[512,2048]{1,0:T(8,128)(2,1)} %sketch_ref.9), channel_id=1, source_target_pairs={{1,0},{2,1},{3,2},{4,3},{5,4},{6,5},{7,6},{8,7},{9,8},{10,9},{11,1... | collective-permute-start | bytes 6291464 | tf_op jit(solution)/shard_map/ppermute | solution.py:231
  17.0 1.6 %copy-start = (bf16[512,2048]{1,0:T(8,128)(2,1)S(1)}, bf16[512,2048]{1,0:T(8,128)(2,1)}, u32[]{:S(2)}) copy-start(bf16[512,2048]{1,0:T(8,128)(2,1)} %sketch_ref.9) | copy-start | bytes 6291460
  18.6 0.7 copy-start.2
  19.7 69.1 %copy-start.3 = (f32[8,512]{1,0:T(8,128)S(1)}, f32[8,512]{1,0:T(8,128)}, u32[]{:S(2)}) copy-start(f32[8,512]{1,0:T(8,128)} %basis_ref.7) | copy-start | bytes 49156
  19.7 72.2 %copy-start.1 = (bf16[512,2048]{1,0:T(8,128)(2,1)S(1)}, bf16[512,2048]{1,0:T(8,128)(2,1)}, u32[]{:S(2)}) copy-start(bf16[512,2048]{1,0:T(8,128)(2,1)} %sketch_ref.9) | copy-start | bytes 6291460
  19.7 8.2 %collective-permute-start.4 = (f32[1,2048]{1,0:T(1,128)S(1)}, f32[1,2048]{1,0:T(1,128)S(1)}, u32[]{:S(2)}, u32[]{:S(2)}) collective-permute-start(f32[1,2048]{1,0:T(1,128)S(1)} %shard_map.54), channel_id=1, source_target_pairs={{1,0},{0,1},{3,2},{2,3},{5,4},{4,5},{7,6},{6,7},{9,8},{8,9},{11,10... | collective-permute-start | bytes 24584 | tf_op jit(solution)/shard_map/ppermute | solution.py:231
  21.8 19.1 %collective-permute-start.5 = (f32[1,2048]{1,0:T(1,128)S(1)}, f32[1,2048]{1,0:T(1,128)S(1)}, u32[]{:S(2)}, u32[]{:S(2)}) collective-permute-start(f32[1,2048]{1,0:T(1,128)S(1)} %shard_map.54), channel_id=1, source_target_pairs={{511,0},{2,1},{1,2},{4,3},{3,4},{6,5},{5,6},{8,7},{7,8},{10,9},{9,... | collective-permute-start | bytes 24584 | tf_op jit(solution)/shard_map/ppermute | solution.py:231
  25.2 15.7 %collective-permute-start.6 = (f32[1,2048]{1,0:T(1,128)S(1)}, f32[1,2048]{1,0:T(1,128)S(1)}, u32[]{:S(2)}, u32[]{:S(2)}) collective-permute-start(f32[1,2048]{1,0:T(1,128)S(1)} %shard_map.54), channel_id=1, source_target_pairs={{128,0},{129,1},{130,2},{131,3},{132,4},{133,5},{134,6},{135,7},{1... | collective-permute-start | bytes 24584 | tf_op jit(solution)/shard_map/ppermute | solution.py:231
  27.9 13.0 %collective-permute-start.7 = (f32[1,2048]{1,0:T(1,128)S(1)}, f32[1,2048]{1,0:T(1,128)S(1)}, u32[]{:S(2)}, u32[]{:S(2)}) collective-permute-start(f32[1,2048]{1,0:T(1,128)S(1)} %shard_map.54), channel_id=1, source_target_pairs={{384,0},{385,1},{386,2},{387,3},{388,4},{389,5},{390,6},{391,7},{3... | collective-permute-start | bytes 24584 | tf_op jit(solution)/shard_map/ppermute | solution.py:231
  52.8 36.1 %all-to-all-start.1 = ((f32[32,8,128]{2,1,0:T(8,128)}), f32[32,8,128]{2,1,0:T(8,128)S(1)}, u32[]{:S(2)}, u32[]{:S(2)}) async-start(f32[32,8,128]{2,1,0:T(8,128)} %broadcast_in_dim.26), calls=%async_computation.1 | async-start | bytes 262144 | tf_op jit(solution)/shard_map/all_to_all | solution.py:219
  95.9 11.1 %collective-permute-start.3 = (bf16[512,512]{1,0:T(8,128)(2,1)S(1)}, bf16[512,512]{1,0:T(8,128)(2,1)S(1)}, u32[]{:S(2)}, u32[]{:S(2)}) collective-permute-start(bf16[512,512]{1,0:T(8,128)(2,1)S(1)} %get-tuple-element.28), channel_id=1, source_target_pairs={{384,0},{129,1},{386,2},{131,3},{388,4},{133,5},{390,6},{135,7},{3... | collective-permute-start | bytes 1572872 | tf_op jit(solution)/shard_map/ppermute | solution.py:231
  103.8 14.7 %collective-permute-start.2 = (bf16[512,512]{1,0:T(8,128)(2,1)S(1)}, bf16[512,512]{1,0:T(8,128)(2,1)S(1)}, u32[]{:S(2)}, u32[]{:S(2)}) collective-permute-start(bf16[512,512]{1,0:T(8,128)(2,1)S(1)} %get-tuple-element.27), channel_id=1, source_target_pairs={{511,0},{0,1},{1,2},{2,3},{3,4},{4,5},{5,6},{6,7},{7,8},{8,9},{9,1... | collective-permute-start | bytes 1572872 | tf_op jit(solution)/shard_map/ppermute | solution.py:231

commit v2 on v0

v2 whole, which is shorter than its diff:
```python
import functools

import jax
import jax.numpy as jnp
import numpy as np
from jax import lax
from jax.experimental import pallas as pl
from jax.experimental.pallas import tpu as pltpu
from jax.sharding import Mesh
from jax.sharding import PartitionSpec as P

AXES = ("x", "z", "y", "core")
SIZES = (4, 8, 8, 2)
FIRST_GROUP = ("z", "core")
SECOND_GROUP = ("x", "y")
BANDS = 5
VMEM_BYTES = 16 * 1024 * 1024
LOAD_VMEM_BYTES = 16 * 1024 * 1024
EXTRA = 16
F32 = jnp.float32
BF16 = jnp.bfloat16


def dot_last(left, right, precision=None):
    return lax.dot_general(
        left, right, (((1,), (1,)), ((), ())), preferred_element_type=F32, precision=precision
    )


def params(**more):
    return pltpu.CompilerParams(vmem_limit_bytes=VMEM_BYTES, **more)


def whole(memory_space=pltpu.VMEM):
    return pl.BlockSpec(memory_space=memory_space)


def shaped(shape, dtype=F32):
    return jax.ShapeDtypeStruct(shape, dtype)


def load_kernel(chunks, sketch_hbm, basis_ref, held_ref, u_ref, sems):
    last = basis_ref.shape[0] - 1
    rows, k = sketch_hbm.shape
    n = rows // chunks
    copies = []
    for i in range(chunks):
        piece = pl.ds(i * n, n)
        copies.append(pltpu.make_async_copy(sketch_hbm.at[piece], held_ref.at[piece], sems.at[i]))
        copies[i].start()
    current = jnp.broadcast_to(basis_ref[last : last + 1, :], (EXTRA, rows))
    held_ref[rows:, :] = jnp.concatenate([current, jnp.zeros((EXTRA, k - rows), F32)], axis=1).astype(BF16)
    total = None
    for i in range(chunks):
        copies[i].wait()
        part = jnp.dot(
            current[:, i * n : (i + 1) * n].astype(BF16),
            held_ref[i * n : (i + 1) * n, :],
            preferred_element_type=F32,
        )
        total = part if total is None else total + part
    u_ref[...] = total[0:1, :]


def load_and_project(sketch, basis):
    chunks = 4
    n, k = sketch.shape
    return pl.pallas_call(
        functools.partial(load_kernel, chunks),
        out_shape=(shaped((n + EXTRA, k), BF16), shaped((1, k))),
        in_specs=[whole(pltpu.HBM), whole()],
        out_specs=(whole(), whole()),
        scratch_shapes=[pltpu.SemaphoreType.DMA((chunks,))],
        compiler_params=pltpu.CompilerParams(vmem_limit_bytes=LOAD_VMEM_BYTES),
        cost_estimate=pl.CostEstimate(
            flops=2 * sketch.size, bytes_accessed=0, transcendentals=0
        ),
    )(sketch, basis)


def pass_kernel(*refs):
    del refs


def after(block, *tokens):
    return pl.pallas_call(
        pass_kernel,
        out_shape=shaped(block.shape, block.dtype),
        in_specs=[whole()] * (1 + len(tokens)),
        out_specs=whole(),
        input_output_aliases={0: 0},
        compiler_params=params(),
    )(block, *tokens)


def own_block_kernel(sketch_ref, basis_ref, rows_ref, own_image_ref, block_ref, sem):
    last = basis_ref.shape[0] - 1
    n = block_ref.shape[0]
    current = basis_ref[last : last + 1, :].astype(BF16)
    sketch = sketch_ref[:n, :]
    block = dot_last(sketch, sketch).astype(BF16)
    block_ref[...] = block
    copy = pltpu.make_async_copy(block_ref, rows_ref.at[:, pl.ds(0, n)], sem)
    copy.start()
    own_image_ref[...] = dot_last(jnp.broadcast_to(current, (16, n)), block)[0:1, :]
    copy.wait()


def own_block(sketch, basis):
    n, k = basis.shape[1], sketch.shape[1]
    return pl.pallas_call(
        own_block_kernel,
        out_shape=(shaped((n, BANDS * n), BF16), shaped((1, n))),
        in_specs=[whole(), whole()],
        out_specs=(whole(pl.ANY), whole()),
        scratch_shapes=[pltpu.VMEM((n, n), BF16), pltpu.SemaphoreType.DMA],
        compiler_params=params(),
        cost_estimate=pl.CostEstimate(
            flops=2 * n * n * k, bytes_accessed=2 * n * k, transcendentals=0
        ),
    )(sketch, basis)


def image_kernel(sketch_ref, mate_ref, basis_ref, own_ref, a_ref, b_ref, c_ref, image_ref, sums_ref):
    rows = own_ref.shape[1]
    mate_u = jnp.dot(mate_ref[rows:, :rows], mate_ref[:rows, :], preferred_element_type=F32)
    total = (a_ref[...] + b_ref[...]) + (c_ref[...] + mate_u[0:1, :])
    high = total.astype(BF16).astype(F32)
    rest = total - high
    middle = rest.astype(BF16).astype(F32)
    low = rest - middle
    row = lax.broadcasted_iota(jnp.int32, (16, total.shape[1]), 0)
    parts = jnp.where(row == 0, high, jnp.where(row == 1, middle, jnp.where(row == 2, low, 0.0)))
    product = dot_last(parts.astype(BF16), sketch_ref[:rows, :])
    image = (product[2:3, :] + product[1:2, :]) + product[0:1, :] + own_ref[...]
    image_ref[...] = image
    basis = basis_ref[...]
    m, n = basis.shape
    place = lax.broadcasted_iota(jnp.int32, (m, n), 0)
    right = jnp.concatenate([basis, jnp.where(place == 0, image, 0.0)] * m, axis=0)
    products = dot_last(basis, right, precision=lax.Precision.HIGHEST)
    norm = jnp.sum(image * image)
    lane = lax.broadcasted_iota(jnp.int32, products.shape, 1)
    line = lax.broadcasted_iota(jnp.int32, products.shape, 0)
    kept = jnp.where((lane // (2 * m)) == line, products, 0.0)
    packed = jnp.sum(kept, axis=0, keepdims=True)
    packed = jnp.where(lane[0:1, :] == m + 1, norm, packed)
    sums_ref[...] = jnp.broadcast_to(packed, sums_ref.shape)


def image_and_sums(sketch, mate, basis, own_image, parts, copies):
    n, k = basis.shape[1], sketch.shape[1]
    return pl.pallas_call(
        image_kernel,
        out_shape=(shaped((1, n)), shaped((copies, 16 * basis.shape[0]))),
        in_specs=[whole()] * 7,
        out_specs=(whole(), whole()),
        compiler_params=params(),
        cost_estimate=pl.CostEstimate(
            flops=2 * n * k * 16, bytes_accessed=2 * n * k, transcendentals=0
        ),
    )(sketch, mate, basis, own_image, *parts)


def add_kernel(rows_ref, copies_ref):
    total = jnp.sum(rows_ref[...], axis=0, keepdims=True)
    copies_ref[...] = jnp.broadcast_to(total, copies_ref.shape)


def add_and_copy(rows, copies):
    return pl.pallas_call(
        add_kernel,
        out_shape=shaped((copies, rows.shape[1])),
        in_specs=[whole()],
        out_specs=whole(),
        compiler_params=params(),
    )(rows)


def plane_rank():
    rank, size = 0, 1
    for name in AXES[1:]:
        rank = rank * lax.axis_size(name) + lax.axis_index(name)
        size = size * lax.axis_size(name)
    return rank, size - 1


def corner_kernel(far_ref, near_ref, token_ref, corner_ref):
    del token_ref
    n = corner_ref.shape[0]
    rank, last = plane_rank()

    @pl.when((rank == 0) | (rank == last))
    def _():
        corner_ref[...] = dot_last(near_ref[:n, :], far_ref[:n, :]).astype(BF16)


def corner_block(far, near, token, n):
    return pl.pallas_call(
        corner_kernel,
        out_shape=shaped((n, n), BF16),
        in_specs=[whole()] * 3,
        out_specs=whole(),
        compiler_params=params(),
    )(far, near, token)


def far_kernel(sketch_ref, far_ref, token_ref, back_ref, block_ref):
    del token_ref
    n = back_ref.shape[0]
    back = dot_last(far_ref[:n, :], sketch_ref[:n, :]).astype(BF16)
    back_ref[...] = back
    block_ref[...] = back.T


def far_blocks(sketch, far, token, n):
    k = sketch.shape[1]
    block = shaped((n, n), BF16)
    return pl.pallas_call(
        far_kernel,
        out_shape=(block, block),
        in_specs=[whole()] * 3,
        out_specs=(whole(), whole()),
        compiler_params=params(),
        cost_estimate=pl.CostEstimate(
            flops=2 * n * n * k, bytes_accessed=4 * n * k, transcendentals=0
        ),
    )(sketch, far, token)


def column_copy(block_ref, rows_ref, column, sem):
    n = block_ref.shape[0]
    start = column * n if isinstance(column, int) else pl.multiple_of(column * n, n)
    return pltpu.make_async_copy(block_ref, rows_ref.at[:, pl.ds(start, n)], sem)


def pairs_kernel(
    sketch_ref, mate_ref, near_ref, far_ref, rows_in_ref, rows_ref, token_ref, blocks_ref, sems
):
    del rows_in_ref
    token_ref[...] = jnp.zeros_like(token_ref)
    n = far_ref.shape[0]
    core = lax.axis_index("core")
    copies = [column_copy(far_ref, rows_ref, 3 + core, sems.at[0])]
    copies[0].start()
    for i, (other_ref, column) in enumerate(((mate_ref, 1 + core), (near_ref, 2 - core))):
        blocks_ref[i] = dot_last(sketch_ref[:n, :], other_ref[:n, :]).astype(BF16)
        copies.append(column_copy(blocks_ref.at[i], rows_ref, column, sems.at[1 + i]))
        copies[-1].start()
    for copy in copies:
        copy.wait()


def pair_blocks(sketch, mate, near, far, rows):
    n, k = far.shape[0], sketch.shape[1]
    return pl.pallas_call(
        pairs_kernel,
        out_shape=(shaped(rows.shape, rows.dtype), shaped((8, 128))),
        in_specs=[whole()] * 4 + [whole(pl.ANY)],
        out_specs=(whole(pl.ANY), whole()),
        scratch_shapes=[pltpu.VMEM((2, n, n), BF16), pltpu.SemaphoreType.DMA((3,))],
        input_output_aliases={4: 0},
        compiler_params=params(),
        cost_estimate=pl.CostEstimate(
            flops=4 * n * n * k, bytes_accessed=4 * n * k, transcendentals=0
        ),
    )(sketch, mate, near, far, rows)


def place_corner_kernel(corner_ref, rows_in_ref, rows_ref, sem):
    del rows_in_ref
    rank, last = plane_rank()

    @pl.when((rank == 0) | (rank == last))
    def _():
        copy = column_copy(corner_ref, rows_ref, jnp.where(rank == 0, 2, 1), sem)
        copy.start()
        copy.wait()


def place_far_kernel(block_ref, rows_in_ref, rows_ref, sem):
    del rows_in_ref
    copy = column_copy(block_ref, rows_ref, 4 - lax.axis_index("core"), sem)
    copy.start()
    copy.wait()


def place(kernel, block, rows):
    n = block.shape[0]
    return pl.pallas_call(
        kernel,
        out_shape=shaped(rows.shape, rows.dtype),
        in_specs=[whole(), whole(pl.ANY)],
        out_specs=whole(pl.ANY),
        scratch_shapes=[pltpu.SemaphoreType.DMA],
        input_output_aliases={1: 0},
        compiler_params=params(),
        cost_estimate=pl.CostEstimate(flops=0, bytes_accessed=4 * n * n, transcendentals=0),
    )(block, rows)


def finish_kernel(count, sums_ref, basis_ref, image_ref, token_ref, left_ref, next_ref, stats_ref, lost_ref):
    del token_ref
    sums = jnp.sum(sums_ref[...], axis=0, keepdims=True)
    basis = basis_ref[...]
    m = basis.shape[0]
    shape = (m, sums.shape[1])
    line = lax.broadcasted_iota(jnp.int32, shape, 0)
    lane = lax.broadcasted_iota(jnp.int32, shape, 1)
    major, minor = lane // (2 * m), lane % (2 * m)
    spread = jnp.broadcast_to(sums, shape)
    inner = jnp.sum(jnp.where((major == line) & (minor == m), spread, 0.0), axis=1, keepdims=True)
    norm = jnp.sum(jnp.where(lane[0:1, :] == m + 1, sums, 0.0), axis=1, keepdims=True)
    coeffs = inner / count
    by_major = jnp.sum(jnp.where(major == line, coeffs, 0.0), axis=0, keepdims=True)
    by_minor = jnp.sum(jnp.where(minor == line, coeffs, 0.0), axis=0, keepdims=True)
    by_lane = jnp.sum(jnp.where(lane == line, coeffs, 0.0), axis=0, keepdims=True)
    quadratic = jnp.sum(sums * by_major * by_minor, axis=1, keepdims=True)
    cross = jnp.sum(coeffs * inner, axis=0, keepdims=True)
    square = (norm - cross) + (quadratic - cross)
    beta = jnp.sqrt(jnp.maximum(square, 0.0) / count + 1e-06)
    left = image_ref[...] - jnp.sum(coeffs * basis, axis=0, keepdims=True)
    left_ref[...] = left
    next_ref[...] = left / beta
    stats_ref[...] = jnp.where(lane[0:1, :] == m, beta, by_lane)
    largest = norm + cross + jnp.abs(quadratic)
    lost_ref[0] = jnp.max(jnp.where(square < 1e-3 * largest, 1.0, 0.0)).astype(jnp.int32)


def finish(sums, basis, image, count, token):
    row = shaped(image.shape)
    return pl.pallas_call(
        functools.partial(finish_kernel, count),
        out_shape=(row, row, shaped((1, 128)), shaped((1,), jnp.int32)),
        in_specs=[whole()] * 4,
        out_specs=(whole(), whole(), whole(), whole(pltpu.SMEM)),
        compiler_params=params(),
    )(sums, basis, image, token)


def group_size(group):
    members = 1
    for name in group:
        members *= lax.axis_size(name)
    return members


def on_device(sketch, basis):
    devices = group_size(AXES)
    stride = devices // SIZES[0]
    total_rows = basis.shape[1] * devices

    def move(block, source_of):
        return lax.ppermute(block, AXES, [(source_of(i) % devices, i) for i in range(devices)])

    def trade(rows, group):
        return lax.all_to_all(rows, group, 0, 0, tiled=True)

    rows_each = sketch.shape[0]
    sketch, u = load_and_project(sketch, basis)
    mate = move(sketch, lambda i: i ^ 1)
    parts = (
        move(u, lambda i: i - 1 if i % 2 == 0 else i + 1),
        move(u, lambda i: i + stride if (i // stride) % 2 == 0 else i - stride),
        move(u, lambda i: i - stride if (i // stride) % 2 == 0 else i + stride),
    )
    sketch = after(sketch, mate, *parts)

    def in_plane(i, step):
        return i // stride * stride + (i + step) % stride

    near = move(sketch, lambda i: in_plane(i, -1 if i % 2 == 0 else 1))
    far = move(sketch, lambda i: i + stride if i % 2 == 0 else i - stride)
    rows, own_image = own_block(sketch, basis)
    image, sums = image_and_sums(sketch, mate, basis, own_image, parts, group_size(FIRST_GROUP))
    sums = add_and_copy(trade(sums, FIRST_GROUP), group_size(SECOND_GROUP))
    sums = trade(sums, SECOND_GROUP)

    corner = corner_block(far, near, sums, rows_each)
    far_back, far_block = far_blocks(sketch, far, corner, rows_each)
    corners = [(i, i + stride - 1) for i in range(0, devices, stride)]
    corner = lax.ppermute(corner, AXES, corners + [(j, i) for i, j in corners])
    far_back = move(far_back, lambda i: i - stride if i % 2 == 0 else i + stride)
    rows, token = pair_blocks(sketch, mate, near, far_block, rows)
    left, next_vector, stats, lost = finish(sums, basis, image, float(total_rows), token)

    m = basis.shape[0]

    def from_sums():
        return next_vector[0], stats[0, : m + 1]

    def from_vector():
        square = lax.psum(jnp.sum(left * left), AXES)
        beta = jnp.sqrt(square / total_rows + 1e-06)
        return left[0] / beta, jnp.concatenate([stats[0, :m], beta[None]])

    next_vector, coefficients = lax.cond(lost[0] != 0, from_vector, from_sums)
    rows = place(place_corner_kernel, corner, rows)
    rows = place(place_far_kernel, far_back, rows)
    return rows, next_vector, coefficients


def solution(mesh):
    grid = Mesh(np.asarray(mesh.devices).reshape(SIZES), AXES)
    return jax.shard_map(
        on_device,
        mesh=grid,
        in_specs=(P(AXES, None), P(None, AXES)),
        out_specs=(P(AXES, None), P(AXES), P()),
        check_vma=False,
    )
```

time: 310 us -> 82.3 us (0.27)
  blocking collectives: 201 us -> 24.6 us
  waiting for transfers between devices: 44.8 us -> 3.47 us
  Pallas kernels: 0 us -> 12.3 us
  matrix products: 11.4 us -> 0 us
  local copies, waits for them, and re-layouts: 9.75 us -> 2.32 us
    psum x2 -> x0, blocking collectives: 201 us -> none  [the longest x1 106 us: on_device(): coeffs = lax.psum(partial_value, 'dp') / total_rows]
    ppermute x8, waiting for transfers between devices: 44.8 us -> 3.47 us  [the longest x1 2.13 us: on_device(): corner = lax.ppermute(corner, AXES, corners + [(j, i) for i, j in corners])]
    all_to_all x0 -> x2, blocking collectives: none -> 24.6 us  [trade(): return lax.all_to_all(rows, group, 0, 0, tiled=True)]
    pallas_call x0 -> x11, Pallas kernels: none -> 12.3 us  [the longest x1 3.19 us: pair_blocks(): pl.pallas_call(pairs_kernel, out_shape=(shaped(rows.shape, rows.dtype), s...]
    dot_general x10 -> x0, matrix products: 11.4 us -> none  [the longest x3 9.16 us: pair_block(): lax.dot_general(left_rows, right_rows, (((1,), (1,)), ((), ())), preferre...]
    convert_element_type x2 -> x0, local copies, waits for them, and re-layouts: 4.12 us -> none  [pair_block(): return lax.dot_general(left_rows, right_rows, (((1,), (1,)), ((), ())), p...]
  transfers between devices with their start and end apart: 8 -> 8, of which waited for: 3 -> 2; matrix products, arithmetic and copies ran while one was open for 5% -> 0% of each run, Pallas kernels for 0% -> 12%
where the time goes in v2:
time: 82.3 us; the launch traced here: 81.3 us
  starting transfers between devices  37.1 us (45%)
  blocking collectives  24.6 us (30%)
  Pallas kernels  12.3 us (15%)
  waiting for transfers between devices  3.47 us (4%)
  local copies, waits for them, and re-layouts  2.32 us (3%)
  between operations  1.47 us (2%)
    ppermute x7, starting transfers between devices, move(): lax.ppermute(block, AXES, [(source_of(i) % devices, i) for i in range(dev...  35.2 us
    all_to_all x2, blocking collectives, trade(): return lax.all_to_all(rows, group, 0, 0, tiled=True)  24.6 us
    pallas_call x1, Pallas kernels, pair_blocks(): pl.pallas_call(pairs_kernel, out_shape=(shaped(rows.shape, rows.dtype), s...  3.19 us
    unnamed x8, local copies, waits for them, and re-layouts  2.31 us
    ppermute x1, waiting for transfers between devices, on_device(): corner = lax.ppermute(corner, AXES, corners + [(j, i) for i, j in corners])  2.13 us
    pallas_call x1, Pallas kernels, own_block(): pl.pallas_call(own_block_kernel, out_shape=(shaped((n, BANDS * n), BF16),...  2.08 us
    ppermute x1, starting transfers between devices, on_device(): corner = lax.ppermute(corner, AXES, corners + [(j, i) for i, j in corners])  1.92 us
  transfers between devices with their start and end apart: 8, of which 2 were waited for; matrix products, arithmetic and copies ran while one was open for 0% of the time, Pallas kernels for 12%

profile of v2, /device:TPU:6, one launch (start us, length us, event | category | flops | bytes accessed | tf_op | source)
XLA Modules:
  0.0 81.3 jit_solution(2888812778443613017)
XLA Ops:
  0.6 0.0 copy-start
  0.6 1.6 %copy-done = bf16[512,2048]{1,0:T(8,128)(2,1)S(1)} copy-done((bf16[512,2048]{1,0:T(8,128)(2,1)S(1)}, bf16[512,2048]{1,0:T(8,128)(2,1)}, u32[]{:S(2)}) %copy-start) | copy-done | bytes 2097176
  2.2 0.0 copy-start.1
  2.2 0.7 copy-done.1
  2.9 0.6 shard_map.49
  3.6 1.9 %collective-permute-start = (bf16[528,2048]{1,0:T(8,128)(2,1)S(1)}, bf16[528,2048]{1,0:T(8,128)(2,1)S(1)}, u32[]{:S(2)}, u32[]{:S(2)}) collective-permute-start(bf16[528,2048]{1,0:T(8,128)(2,1)S(1)} %get-tuple-element.31.refs_0_), channel_id=1, source_target_pairs={{1,0},{0,1},{3,2},{2,3},{5,4},{4,5},{7,6},{6,7},{9,8},{8,9},{11,10... | collective-permute-start | bytes 6488072 | tf_op jit(solution)/shard_map/ppermute | solution.py:354
  5.5 7.8 %collective-permute-start.3 = (f32[1,2048]{1,0:T(1,128)S(1)}, f32[1,2048]{1,0:T(1,128)S(1)}, u32[]{:S(2)}, u32[]{:S(2)}) collective-permute-start(f32[1,2048]{1,0:T(1,128)S(1)} %get-tuple-element.32), channel_id=1, source_target_pairs={{384,0},{385,1},{386,2},{387,3},{388,4},{389,5},{390,6},{391,7},{3... | collective-permute-start | bytes 24584 | tf_op jit(solution)/shard_map/ppermute | solution.py:354
  13.3 1.9 %collective-permute-start.2 = (f32[1,2048]{1,0:T(1,128)S(1)}, f32[1,2048]{1,0:T(1,128)S(1)}, u32[]{:S(2)}, u32[]{:S(2)}) collective-permute-start(f32[1,2048]{1,0:T(1,128)S(1)} %get-tuple-element.32), channel_id=1, source_target_pairs={{128,0},{129,1},{130,2},{131,3},{132,4},{133,5},{134,6},{135,7},{1... | collective-permute-start | bytes 24584 | tf_op jit(solution)/shard_map/ppermute | solution.py:354
  15.2 9.5 %collective-permute-start.1 = (f32[1,2048]{1,0:T(1,128)S(1)}, f32[1,2048]{1,0:T(1,128)S(1)}, u32[]{:S(2)}, u32[]{:S(2)}) collective-permute-start(f32[1,2048]{1,0:T(1,128)S(1)} %get-tuple-element.32), channel_id=1, source_target_pairs={{511,0},{2,1},{1,2},{4,3},{3,4},{6,5},{5,6},{8,7},{7,8},{10,9},{9,... | collective-permute-start | bytes 24584 | tf_op jit(solution)/shard_map/ppermute | solution.py:354
  24.7 0.0 collective-permute-done.3.refs_4_.c_ref
  24.7 0.0 collective-permute-done.2.refs_3_.b_ref
  24.7 1.3 %collective-permute-done.1.refs_2_.a_ref = f32[1,2048]{1,0:T(1,128)S(1)} collective-permute-done((f32[1,2048]{1,0:T(1,128)S(1)}, f32[1,2048]{1,0:T(1,128)S(1)}, u32[]{:S(2)}, u32[]{:S(2)}) %collective-permute-start.1) | collective-permute-done | bytes 8224 | tf_op jit(solution)/shard_map/ppermute | solution.py:354
  26.0 0.0 collective-permute-done.refs_1_.mate_ref
  26.0 8.5 %collective-permute-start.5 = (bf16[528,2048]{1,0:T(8,128)(2,1)S(1)}, bf16[528,2048]{1,0:T(8,128)(2,1)S(1)}, u32[]{:S(2)}, u32[]{:S(2)}) collective-permute-start(bf16[528,2048]{1,0:T(8,128)(2,1)S(1)} %shard_map.50.sketch_ref), channel_id=1, source_target_pairs={{127,0},{2,1},{1,2},{4,3},{3,4},{6,5},{5,6},{8,7},{7,8},{10,9},{9,... | collective-permute-start | bytes 6488072 | tf_op jit(solution)/shard_map/ppermute | solution.py:354
  34.5 1.9 %collective-permute-start.4 = (bf16[528,2048]{1,0:T(8,128)(2,1)S(1)}, bf16[528,2048]{1,0:T(8,128)(2,1)S(1)}, u32[]{:S(2)}, u32[]{:S(2)}) collective-permute-start(bf16[528,2048]{1,0:T(8,128)(2,1)S(1)} %shard_map.50.sketch_ref), channel_id=1, source_target_pairs={{128,0},{385,1},{130,2},{387,3},{132,4},{389,5},{134,6},{391,7},{1... | collective-permute-start | bytes 6488072 | tf_op jit(solution)/shard_map/ppermute | solution.py:354
  36.4 2.1 %shard_map.51 = (bf16[512,2560]{1,0:T(8,128)(2,1)}, f32[1,512]{1,0:T(1,128)S(1)}) custom-call(bf16[528,2048]{1,0:T(8,128)(2,1)S(1)} %shard_map.50.sketch_ref, f32[8,512]{1,0:T(8,128)S(1)} %copy-done.1), custom_call_target="tpu_custom_call" | custom-call | flops 1073741824 | bytes 2097152 | tf_op jit(solution)/shard_map/pallas_call | solution.py:111
  38.5 1.4 %shard_map.52 = (f32[1,512]{1,0:T(1,128)S(1)}, f32[16,128]{1,0:T(8,128)S(1)}) custom-call(bf16[528,2048]{1,0:T(8,128)(2,1)S(1)} %shard_map.50.sketch_ref, bf16[528,2048]{1,0:T(8,128)(2,1)S(1)} %collective-permute-done.refs_1_.mate_ref, f32[8,512]{1,0:T(8,128)S(1)} %copy-done.1, f32[1,512]{1,0:T(1,128)S(1)} %get-tuple-element.33.own_ref, ...), custom_call_target="tpu_custom_call" | custom-call | flops 33554432 | bytes 2097152 | tf_op jit(solution)/shard_map/pallas_call | solution.py:153
  39.9 10.5 %all_to_all.22 = f32[16,1,128]{2,1,0:T(1,128)S(1)} all-to-all(f32[16,1,128]{2,1,0:T(1,128)S(1)} %bitcast.19), channel_id=1, replica_groups=mesh['x'=4,'z'=8,'y'=8,'core'=2] {'z','core'}, dimensions={0} | all-to-all | bytes 16384 | tf_op jit(solution)/shard_map/all_to_all | solution.py:357
  50.4 14.1 %all_to_all.23 = f32[32,1,128]{2,1,0:T(1,128)S(1)} all-to-all(f32[32,1,128]{2,1,0:T(1,128)S(1)} %bitcast.17), channel_id=1, replica_groups=mesh['x'=4,'z'=8,'y'=8,'core'=2] {'x','y'}, dimensions={0} | all-to-all | bytes 32768 | tf_op jit(solution)/shard_map/all_to_all | solution.py:357
  64.6 0.0 collective-permute-done.5.near_ref
  64.6 0.0 collective-permute-done.4.far_ref
  64.6 1.3 %shard_map.54.token_ref = bf16[512,512]{1,0:T(8,128)(2,1)S(1)} custom-call(bf16[528,2048]{1,0:T(8,128)(2,1)S(1)} %collective-permute-done.4.far_ref, bf16[528,2048]{1,0:T(8,128)(2,1)S(1)} %collective-permute-done.5.near_ref, f32[32,128]{1,0:T(8,128)S(1)} %bitcast.15), custom_call_target="tpu_custom_call" | custom-call | tf_op jit(solution)/shard_map/pallas_call | solution.py:199
  65.8 1.9 %collective-permute-start.7 = (bf16[512,512]{1,0:T(8,128)(2,1)S(1)}, bf16[512,512]{1,0:T(8,128)(2,1)S(1)}, u32[]{:S(2)}, u32[]{:S(2)}) collective-permute-start(bf16[512,512]{1,0:T(8,128)(2,1)S(1)} %shard_map.54.token_ref), channel_id=1, source_target_pairs={{0,127},{128,255},{256,383},{384,511},{127,0},{255,128},{383,256},... | collective-permute-start | bytes 1572872 | tf_op jit(solution)/shard_map/ppermute | solution.py:382
  67.8 1.4 %shard_map.55 = (bf16[512,512]{1,0:T(8,128)(2,1)S(1)}, bf16[512,512]{1,0:T(8,128)(2,1)S(1)}) custom-call(bf16[528,2048]{1,0:T(8,128)(2,1)S(1)} %shard_map.50.sketch_ref, bf16[528,2048]{1,0:T(8,128)(2,1)S(1)} %collective-permute-done.4.far_ref, bf16[512,512]{1,0:T(8,128)(2,1)S(1)} %shard_map.54.token_ref), custom_call_target="tpu_custom_call" | custom-call | flops 1073741824 | bytes 4194304 | tf_op jit(solution)/shard_map/pallas_call | solution.py:219
  69.1 3.8 %collective-permute-start.6 = (bf16[512,512]{1,0:T(8,128)(2,1)S(1)}, bf16[512,512]{1,0:T(8,128)(2,1)S(1)}, u32[]{:S(2)}, u32[]{:S(2)}) collective-permute-start(bf16[512,512]{1,0:T(8,128)(2,1)S(1)} %get-tuple-element.35), channel_id=1, source_target_pairs={{384,0},{129,1},{386,2},{131,3},{388,4},{133,5},{390,6},{135,7},{3... | collective-permute-start | bytes 1572872 | tf_op jit(solution)/shard_map/ppermute | solution.py:354
  72.9 3.2 %shard_map.56 = (bf16[512,2560]{1,0:T(8,128)(2,1)}, f32[8,128]{1,0:T(8,128)S(1)}) custom-call(bf16[528,2048]{1,0:T(8,128)(2,1)S(1)} %shard_map.50.sketch_ref, bf16[528,2048]{1,0:T(8,128)(2,1)S(1)} %collective-permute-done.refs_1_.mate_ref, bf16[528,2048]{1,0:T(8,128)(2,1)S(1)} %collective-permute-done.5.near_ref, ...), custom_call_target="tpu_custom_call", output_to_operand_aliasing={{0}: (4, {})} | custom-call | flops 2147483648 | bytes 4194304 | tf_op jit(solution)/shard_map/pallas_call | solution.py:256
  76.1 0.7 shard_map.59
  77.5 0.0 copy-start.2
  77.5 0.0 copy-start.3
  77.5 2.1 %collective-permute-done.7.corner_ref = bf16[512,512]{1,0:T(8,128)(2,1)S(1)} collective-permute-done((bf16[512,512]{1,0:T(8,128)(2,1)S(1)}, bf16[512,512]{1,0:T(8,128)(2,1)S(1)}, u32[]{:S(2)}, u32[]{:S(2)}) %collective-permute-start.7) | collective-permute-done | bytes 524320 | tf_op jit(solution)/shard_map/ppermute | solution.py:382
  79.7 0.8 shard_map.57.rows_in_ref
  80.5 0.0 copy-done.2
  80.5 0.0 copy-done.3
  80.5 0.0 collective-permute-done.6.block_ref
  80.5 0.8 %shard_map.58 = bf16[512,2560]{1,0:T(8,128)(2,1)} custom-call(bf16[512,512]{1,0:T(8,128)(2,1)S(1)} %collective-permute-done.6.block_ref, bf16[512,2560]{1,0:T(8,128)(2,1)} %shard_map.57.rows_in_ref), custom_call_target="tpu_custom_call", output_to_operand_aliasing={{}: (1, {})} | custom-call | bytes 1048576 | tf_op jit(solution)/shard_map/pallas_call | solution.py:290
  (4 shorter events, 0.0 us)
Async XLA Ops:
  0.6 1.6 %copy-start = (bf16[512,2048]{1,0:T(8,128)(2,1)S(1)}, bf16[512,2048]{1,0:T(8,128)(2,1)}, u32[]{:S(2)}) copy-start(bf16[512,2048]{1,0:T(8,128)(2,1)} %sketch_hbm.1) | copy-start | bytes 6291460
  2.2 0.7 copy-start.1
  3.6 22.5 %collective-permute-start = (bf16[528,2048]{1,0:T(8,128)(2,1)S(1)}, bf16[528,2048]{1,0:T(8,128)(2,1)S(1)}, u32[]{:S(2)}, u32[]{:S(2)}) collective-permute-start(bf16[528,2048]{1,0:T(8,128)(2,1)S(1)} %get-tuple-element.31.refs_0_), channel_id=1, source_target_pairs={{1,0},{0,1},{3,2},{2,3},{5,4},{4,5},{7,6},{6,7},{9,8},{8,9},{11,10... | collective-permute-start | bytes 6488072 | tf_op jit(solution)/shard_map/ppermute | solution.py:354
  5.5 19.2 %collective-permute-start.3 = (f32[1,2048]{1,0:T(1,128)S(1)}, f32[1,2048]{1,0:T(1,128)S(1)}, u32[]{:S(2)}, u32[]{:S(2)}) collective-permute-start(f32[1,2048]{1,0:T(1,128)S(1)} %get-tuple-element.32), channel_id=1, source_target_pairs={{384,0},{385,1},{386,2},{387,3},{388,4},{389,5},{390,6},{391,7},{3... | collective-permute-start | bytes 24584 | tf_op jit(solution)/shard_map/ppermute | solution.py:354
  13.3 11.4 %collective-permute-start.2 = (f32[1,2048]{1,0:T(1,128)S(1)}, f32[1,2048]{1,0:T(1,128)S(1)}, u32[]{:S(2)}, u32[]{:S(2)}) collective-permute-start(f32[1,2048]{1,0:T(1,128)S(1)} %get-tuple-element.32), channel_id=1, source_target_pairs={{128,0},{129,1},{130,2},{131,3},{132,4},{133,5},{134,6},{135,7},{1... | collective-permute-start | bytes 24584 | tf_op jit(solution)/shard_map/ppermute | solution.py:354
  15.2 10.8 %collective-permute-start.1 = (f32[1,2048]{1,0:T(1,128)S(1)}, f32[1,2048]{1,0:T(1,128)S(1)}, u32[]{:S(2)}, u32[]{:S(2)}) collective-permute-start(f32[1,2048]{1,0:T(1,128)S(1)} %get-tuple-element.32), channel_id=1, source_target_pairs={{511,0},{2,1},{1,2},{4,3},{3,4},{6,5},{5,6},{8,7},{7,8},{10,9},{9,... | collective-permute-start | bytes 24584 | tf_op jit(solution)/shard_map/ppermute | solution.py:354
  26.0 38.5 %collective-permute-start.5 = (bf16[528,2048]{1,0:T(8,128)(2,1)S(1)}, bf16[528,2048]{1,0:T(8,128)(2,1)S(1)}, u32[]{:S(2)}, u32[]{:S(2)}) collective-permute-start(bf16[528,2048]{1,0:T(8,128)(2,1)S(1)} %shard_map.50.sketch_ref), channel_id=1, source_target_pairs={{127,0},{2,1},{1,2},{4,3},{3,4},{6,5},{5,6},{8,7},{7,8},{10,9},{9,... | collective-permute-start | bytes 6488072 | tf_op jit(solution)/shard_map/ppermute | solution.py:354
  34.5 30.1 %collective-permute-start.4 = (bf16[528,2048]{1,0:T(8,128)(2,1)S(1)}, bf16[528,2048]{1,0:T(8,128)(2,1)S(1)}, u32[]{:S(2)}, u32[]{:S(2)}) collective-permute-start(bf16[528,2048]{1,0:T(8,128)(2,1)S(1)} %shard_map.50.sketch_ref), channel_id=1, source_target_pairs={{128,0},{385,1},{130,2},{387,3},{132,4},{389,5},{134,6},{391,7},{1... | collective-permute-start | bytes 6488072 | tf_op jit(solution)/shard_map/ppermute | solution.py:354
  65.8 13.8 %collective-permute-start.7 = (bf16[512,512]{1,0:T(8,128)(2,1)S(1)}, bf16[512,512]{1,0:T(8,128)(2,1)S(1)}, u32[]{:S(2)}, u32[]{:S(2)}) collective-permute-start(bf16[512,512]{1,0:T(8,128)(2,1)S(1)} %shard_map.54.token_ref), channel_id=1, source_target_pairs={{0,127},{128,255},{256,383},{384,511},{127,0},{255,128},{383,256},... | collective-permute-start | bytes 1572872 | tf_op jit(solution)/shard_map/ppermute | solution.py:382
  69.1 11.4 %collective-permute-start.6 = (bf16[512,512]{1,0:T(8,128)(2,1)S(1)}, bf16[512,512]{1,0:T(8,128)(2,1)S(1)}, u32[]{:S(2)}, u32[]{:S(2)}) collective-permute-start(bf16[512,512]{1,0:T(8,128)(2,1)S(1)} %get-tuple-element.35), channel_id=1, source_target_pairs={{384,0},{129,1},{386,2},{131,3},{388,4},{133,5},{390,6},{135,7},{3... | collective-permute-start | bytes 1572872 | tf_op jit(solution)/shard_map/ppermute | solution.py:354
  77.5 3.0 %copy-start.2 = (f32[1,512]{1,0:T(1,128)}, f32[1,512]{1,0:T(1,128)S(1)}, u32[]{:S(2)}) copy-start(f32[1,512]{1,0:T(1,128)S(1)} %get-tuple-element.48) | copy-start | bytes 6148
  77.5 3.0 %copy-start.3 = (f32[9]{0:T(128)}, f32[9]{0:T(128)S(1)}, u32[]{:S(2)}) copy-start(f32[9]{0:T(128)S(1)} %get-tuple-element.30) | copy-start | bytes 112

commit v3 on v2

--- a/solution.py
+++ b/solution.py
@@ -39,15 +39,18 @@
     return jax.ShapeDtypeStruct(shape, dtype)
 
 
-def load_kernel(chunks, sketch_hbm, basis_ref, held_ref, u_ref, sems):
+def load_kernel(chunks, sketch_hbm, basis_hbm, held_ref, u_ref, basis_ref, sems):
     last = basis_ref.shape[0] - 1
     rows, k = sketch_hbm.shape
     n = rows // chunks
+    basis_copy = pltpu.make_async_copy(basis_hbm, basis_ref, sems.at[chunks])
+    basis_copy.start()
     copies = []
     for i in range(chunks):
         piece = pl.ds(i * n, n)
         copies.append(pltpu.make_async_copy(sketch_hbm.at[piece], held_ref.at[piece], sems.at[i]))
         copies[i].start()
+    basis_copy.wait()
     current = jnp.broadcast_to(basis_ref[last : last + 1, :], (EXTRA, rows))
     held_ref[rows:, :] = jnp.concatenate([current, jnp.zeros((EXTRA, k - rows), F32)], axis=1).astype(BF16)
     total = None
@@ -67,10 +70,10 @@
     n, k = sketch.shape
     return pl.pallas_call(
         functools.partial(load_kernel, chunks),
-        out_shape=(shaped((n + EXTRA, k), BF16), shaped((1, k))),
-        in_specs=[whole(pltpu.HBM), whole()],
-        out_specs=(whole(), whole()),
-        scratch_shapes=[pltpu.SemaphoreType.DMA((chunks,))],
+        out_shape=(shaped((n + EXTRA, k), BF16), shaped((1, k)), shaped(basis.shape)),
+        in_specs=[whole(pltpu.HBM), whole(pltpu.HBM)],
+        out_specs=(whole(), whole(), whole()),
+        scratch_shapes=[pltpu.SemaphoreType.DMA((chunks + 1,))],
         compiler_params=pltpu.CompilerParams(vmem_limit_bytes=LOAD_VMEM_BYTES),
         cost_estimate=pl.CostEstimate(
             flops=2 * sketch.size, bytes_accessed=0, transcendentals=0
@@ -78,19 +81,21 @@
     )(sketch, basis)
 
 
-def pass_kernel(*refs):
-    del refs
-
-
-def after(block, *tokens):
-    return pl.pallas_call(
-        pass_kernel,
-        out_shape=shaped(block.shape, block.dtype),
-        in_specs=[whole()] * (1 + len(tokens)),
+def mate_kernel(mate_ref, u_ref):
+    n = mate_ref.shape[0] - EXTRA
+    product = jnp.dot(mate_ref[n:, :n], mate_ref[:n, :], preferred_element_type=F32)
+    u_ref[...] = product[0:1, :]
+
+
+def mate_projection(mate):
+    return pl.pallas_call(
+        mate_kernel,
+        out_shape=shaped((1, mate.shape[1])),
+        in_specs=[whole()],
         out_specs=whole(),
-        input_output_aliases={0: 0},
-        compiler_params=params(),
-    )(block, *tokens)
+        compiler_params=params(),
+        cost_estimate=pl.CostEstimate(flops=2 * mate.size, bytes_accessed=2 * mate.size, transcendentals=0),
+    )(mate)
 
 
 def own_block_kernel(sketch_ref, basis_ref, rows_ref, own_image_ref, block_ref, sem):
@@ -121,10 +126,9 @@
     )(sketch, basis)
 
 
-def image_kernel(sketch_ref, mate_ref, basis_ref, own_ref, a_ref, b_ref, c_ref, image_ref, sums_ref):
+def image_kernel(sketch_ref, basis_ref, own_ref, a_ref, b_ref, c_ref, d_ref, image_ref, sums_ref):
     rows = own_ref.shape[1]
-    mate_u = jnp.dot(mate_ref[rows:, :rows], mate_ref[:rows, :], preferred_element_type=F32)
-    total = (a_ref[...] + b_ref[...]) + (c_ref[...] + mate_u[0:1, :])
+    total = (a_ref[...] + b_ref[...]) + (c_ref[...] + d_ref[...])
     high = total.astype(BF16).astype(F32)
     rest = total - high
     middle = rest.astype(BF16).astype(F32)
@@ -148,7 +152,7 @@
     sums_ref[...] = jnp.broadcast_to(packed, sums_ref.shape)
 
 
-def image_and_sums(sketch, mate, basis, own_image, parts, copies):
+def image_and_sums(sketch, basis, own_image, parts, copies):
     n, k = basis.shape[1], sketch.shape[1]
     return pl.pallas_call(
         image_kernel,
@@ -159,7 +163,7 @@
         cost_estimate=pl.CostEstimate(
             flops=2 * n * k * 16, bytes_accessed=2 * n * k, transcendentals=0
         ),
-    )(sketch, mate, basis, own_image, *parts)
+    )(sketch, basis, own_image, *parts)
 
 
 def add_kernel(rows_ref, copies_ref):
@@ -187,12 +191,11 @@
 
 def corner_kernel(far_ref, near_ref, token_ref, corner_ref):
     del token_ref
-    n = corner_ref.shape[0]
     rank, last = plane_rank()
 
     @pl.when((rank == 0) | (rank == last))
     def _():
-        corner_ref[...] = dot_last(near_ref[:n, :], far_ref[:n, :]).astype(BF16)
+        corner_ref[...] = dot_last(far_ref[...], near_ref[...]).astype(BF16)
 
 
 def corner_block(far, near, token, n):
@@ -208,7 +211,7 @@
 def far_kernel(sketch_ref, far_ref, token_ref, back_ref, block_ref):
     del token_ref
     n = back_ref.shape[0]
-    back = dot_last(far_ref[:n, :], sketch_ref[:n, :]).astype(BF16)
+    back = dot_last(far_ref[...], sketch_ref[:n, :]).astype(BF16)
     back_ref[...] = back
     block_ref[...] = back.T
 
@@ -235,68 +238,49 @@
 
 
 def pairs_kernel(
-    sketch_ref, mate_ref, near_ref, far_ref, rows_in_ref, rows_ref, token_ref, blocks_ref, sems
+    sketch_ref, mate_ref, near_ref, far_ref, back_ref, corner_ref, sums_ref, rows_in_ref,
+    rows_ref, token_ref, blocks_ref, sems,
 ):
-    del rows_in_ref
+    del sums_ref, rows_in_ref
     token_ref[...] = jnp.zeros_like(token_ref)
     n = far_ref.shape[0]
     core = lax.axis_index("core")
-    copies = [column_copy(far_ref, rows_ref, 3 + core, sems.at[0])]
-    copies[0].start()
-    for i, (other_ref, column) in enumerate(((mate_ref, 1 + core), (near_ref, 2 - core))):
-        blocks_ref[i] = dot_last(sketch_ref[:n, :], other_ref[:n, :]).astype(BF16)
-        copies.append(column_copy(blocks_ref.at[i], rows_ref, column, sems.at[1 + i]))
-        copies[-1].start()
+    rank, last = plane_rank()
+    copies = [
+        column_copy(far_ref, rows_ref, 3 + core, sems.at[0]),
+        column_copy(back_ref, rows_ref, 4 - core, sems.at[1]),
+    ]
+    for copy in copies:
+        copy.start()
+    blocks_ref[0] = dot_last(sketch_ref[:n, :], mate_ref[:n, :]).astype(BF16)
+    copies.append(column_copy(blocks_ref.at[0], rows_ref, 1 + core, sems.at[2]))
+    copies[-1].start()
+    blocks_ref[1] = dot_last(sketch_ref[:n, :], near_ref[...]).astype(BF16)
+
+    @pl.when((rank == 0) | (rank == last))
+    def _():
+        blocks_ref[1] = corner_ref[...]
+
+    copies.append(column_copy(blocks_ref.at[1], rows_ref, 2 - core, sems.at[3]))
+    copies[-1].start()
     for copy in copies:
         copy.wait()
 
 
-def pair_blocks(sketch, mate, near, far, rows):
-    n, k = far.shape[0], sketch.shape[1]
+def pair_blocks(sketch, mate, near, far, back, corner, sums, rows):
+    n, k = near.shape
     return pl.pallas_call(
         pairs_kernel,
         out_shape=(shaped(rows.shape, rows.dtype), shaped((8, 128))),
-        in_specs=[whole()] * 4 + [whole(pl.ANY)],
+        in_specs=[whole()] * 7 + [whole(pl.ANY)],
         out_specs=(whole(pl.ANY), whole()),
-        scratch_shapes=[pltpu.VMEM((2, n, n), BF16), pltpu.SemaphoreType.DMA((3,))],
-        input_output_aliases={4: 0},
+        scratch_shapes=[pltpu.VMEM((2, n, n), BF16), pltpu.SemaphoreType.DMA((4,))],
+        input_output_aliases={7: 0},
         compiler_params=params(),
         cost_estimate=pl.CostEstimate(
             flops=4 * n * n * k, bytes_accessed=4 * n * k, transcendentals=0
         ),
-    )(sketch, mate, near, far, rows)
-
-
-def place_corner_kernel(corner_ref, rows_in_ref, rows_ref, sem):
-    del rows_in_ref
-    rank, last = plane_rank()
-
-    @pl.when((rank == 0) | (rank == last))
-    def _():
-        copy = column_copy(corner_ref, rows_ref, jnp.where(rank == 0, 2, 1), sem)
-        copy.start()
-        copy.wait()
-
-
-def place_far_kernel(block_ref, rows_in_ref, rows_ref, sem):
-    del rows_in_ref
-    copy = column_copy(block_ref, rows_ref, 4 - lax.axis_index("core"), sem)
-    copy.start()
-    copy.wait()
-
-
-def place(kernel, block, rows):
-    n = block.shape[0]
-    return pl.pallas_call(
-        kernel,
-        out_shape=shaped(rows.shape, rows.dtype),
-        in_specs=[whole(), whole(pl.ANY)],
-        out_specs=whole(pl.ANY),
-        scratch_shapes=[pltpu.SemaphoreType.DMA],
-        input_output_aliases={1: 0},
-        compiler_params=params(),
-        cost_estimate=pl.CostEstimate(flops=0, bytes_accessed=4 * n * n, transcendentals=0),
-    )(block, rows)
+    )(sketch, mate, near, far, back, corner, sums, rows)
 
 
 def finish_kernel(count, sums_ref, basis_ref, image_ref, token_ref, left_ref, next_ref, stats_ref, lost_ref):
@@ -357,31 +341,35 @@
         return lax.all_to_all(rows, group, 0, 0, tiled=True)
 
     rows_each = sketch.shape[0]
-    sketch, u = load_and_project(sketch, basis)
-    mate = move(sketch, lambda i: i ^ 1)
-    parts = (
-        move(u, lambda i: i - 1 if i % 2 == 0 else i + 1),
-        move(u, lambda i: i + stride if (i // stride) % 2 == 0 else i - stride),
-        move(u, lambda i: i - stride if (i // stride) % 2 == 0 else i + stride),
-    )
-    sketch = after(sketch, mate, *parts)
 
     def in_plane(i, step):
         return i // stride * stride + (i + step) % stride
 
+    far = move(sketch, lambda i: i + stride if i % 2 == 0 else i - stride)
     near = move(sketch, lambda i: in_plane(i, -1 if i % 2 == 0 else 1))
-    far = move(sketch, lambda i: i + stride if i % 2 == 0 else i - stride)
+    stored = [pltpu.with_memory_space_constraint(array, pltpu.HBM) for array in (sketch, basis)]
+    sketch, u, basis = load_and_project(*stored)
+    mate = move(sketch, lambda i: i ^ 1)
+    mate_u = mate_projection(mate)
+    parts = (
+        move(u, lambda i: i - stride if i % 2 == 0 else i + stride),
+        move(mate_u, lambda i: i + stride + 1 if i % 2 == 0 else i - stride - 1),
+        move(mate_u, lambda i: i - 2 if i % 2 == 0 else i + 2),
+        mate_u,
+    )
     rows, own_image = own_block(sketch, basis)
-    image, sums = image_and_sums(sketch, mate, basis, own_image, parts, group_size(FIRST_GROUP))
+    image, sums = image_and_sums(sketch, basis, own_image, parts, group_size(FIRST_GROUP))
     sums = add_and_copy(trade(sums, FIRST_GROUP), group_size(SECOND_GROUP))
-    sums = trade(sums, SECOND_GROUP)
-
     corner = corner_block(far, near, sums, rows_each)
     far_back, far_block = far_blocks(sketch, far, corner, rows_each)
-    corners = [(i, i + stride - 1) for i in range(0, devices, stride)]
-    corner = lax.ppermute(corner, AXES, corners + [(j, i) for i, j in corners])
-    far_back = move(far_back, lambda i: i - stride if i % 2 == 0 else i + stride)
-    rows, token = pair_blocks(sketch, mate, near, far_block, rows)
+    def to_sender(i):
+        return (i + stride if i % 2 == 0 else i - stride) % devices
+
+    corners = [i for i in range(devices) if i % stride in (0, stride - 1)]
+    corner = lax.ppermute(corner, AXES, [(i, to_sender(i)) for i in corners] + [(2, 4)])
+    far_back = lax.ppermute(far_back, AXES, [(i, to_sender(i)) for i in range(devices)])
+    sums = trade(sums, SECOND_GROUP)
+    rows, token = pair_blocks(sketch, mate, near, far_block, far_back, corner, sums, rows)
     left, next_vector, stats, lost = finish(sums, basis, image, float(total_rows), token)
 
     m = basis.shape[0]
@@ -395,8 +383,6 @@
         return left[0] / beta, jnp.concatenate([stats[0, :m], beta[None]])
 
     next_vector, coefficients = lax.cond(lost[0] != 0, from_vector, from_sums)
-    rows = place(place_corner_kernel, corner, rows)
-    rows = place(place_far_kernel, far_back, rows)
     return rows, next_vector, coefficients
 
 

time: 82.3 us -> 75.1 us (0.913)
  starting transfers between devices: 37.1 us -> 33.9 us
  local copies, waits for them, and re-layouts: 2.32 us -> 0.57 us
  waiting for transfers between devices: 3.47 us -> 1.82 us
    ppermute x7 -> x6, starting transfers between devices: 35.2 us -> 27.4 us  [move(): lax.ppermute(block, AXES, [(source_of(i) % devices, i) for i in range(dev...]
    ppermute x1 -> x2, starting transfers between devices: 1.92 us -> 6.5 us  [the longest x1 4.58 us: on_device(): lax.ppermute(far_back, AXES, [(i, to_sender(i)) for i in range(devices)])]
    ppermute x1 -> x2, waiting for transfers between devices: 2.13 us -> 0.01 us  [the longest x1 0.01 us: on_device(): lax.ppermute(far_back, AXES, [(i, to_sender(i)) for i in range(devices)])]
    unnamed x8 -> x4, local copies, waits for them, and re-layouts: 2.31 us -> 0.57 us
    pallas_call x3 -> x1, Pallas kernels: 1.61 us -> 0.38 us  [mate_projection(): pl.pallas_call(mate_kernel, out_shape=shaped((1, mate.shape[1])), in_spec...]
    pallas_call x1, Pallas kernels: 0.61 us -> 1.76 us  [load_and_project(): pl.pallas_call(functools.partial(load_kernel, chunks), out_shape=(shaped(...]
    ppermute x7 -> x6, waiting for transfers between devices: 1.34 us -> 1.81 us  [move(): lax.ppermute(block, AXES, [(source_of(i) % devices, i) for i in range(dev...]
  transfers between devices with their start and end apart: 8 -> 8, of which waited for: 2 -> 1; matrix products, arithmetic and copies ran while one was open for 0% -> 0% of each run, Pallas kernels for 12% -> 5%
where the time goes in v3:
time: 75.1 us; the launch traced here: 73.9 us
  starting transfers between devices  33.9 us (45%)
  blocking collectives  24 us (32%)
  Pallas kernels  12.2 us (16%)
  waiting for transfers between devices  1.82 us (2%)
  between operations  1.44 us (2%)
    ppermute x6, starting transfers between devices, move(): lax.ppermute(block, AXES, [(source_of(i) % devices, i) for i in range(dev...  27.4 us
    all_to_all x2, blocking collectives, trade(): return lax.all_to_all(rows, group, 0, 0, tiled=True)  24 us
    ppermute x1, starting transfers between devices, on_device(): lax.ppermute(far_back, AXES, [(i, to_sender(i)) for i in range(devices)])  4.58 us
    pallas_call x1, Pallas kernels, pair_blocks(): pl.pallas_call(pairs_kernel, out_shape=(shaped(rows.shape, rows.dtype), s...  3.39 us
    pallas_call x1, Pallas kernels, own_block(): pl.pallas_call(own_block_kernel, out_shape=(shaped((n, BANDS * n), BF16),...  2.09 us
    ppermute x1, starting transfers between devices, on_device(): lax.ppermute(corner, AXES, [(i, to_sender(i)) for i in corners] + [(2, 4)])  1.92 us
    ppermute x6, waiting for transfers between devices, move(): lax.ppermute(block, AXES, [(source_of(i) % devices, i) for i in range(dev...  1.81 us
    pallas_call x1, Pallas kernels, load_and_project(): pl.pallas_call(functools.partial(load_kernel, chunks), out_shape=(shaped(...  1.76 us
  transfers between devices with their start and end apart: 8, of which 1 were waited for; matrix products, arithmetic and copies ran while one was open for 0% of the time, Pallas kernels for 5%

profile of v3, /device:TPU:6, one launch (start us, length us, event | category | flops | bytes accessed | tf_op | source)
XLA Modules:
  0.0 73.9 jit_solution(5857666716396084417)
XLA Ops:
  0.6 1.8 %shard_map.49 = (bf16[528,2048]{1,0:T(8,128)(2,1)S(1)}, f32[1,2048]{1,0:T(1,128)S(1)}, f32[8,512]{1,0:T(8,128)S(1)}) custom-call(bf16[512,2048]{1,0:T(8,128)(2,1)} %sketch_hbm.1, f32[8,512]{1,0:T(8,128)} %basis_hbm.1), custom_call_target="tpu_custom_call" | custom-call | flops 2097152 | tf_op jit(solution)/shard_map/pallas_call | solution.py:71
  2.4 1.9 %collective-permute-start = (bf16[528,2048]{1,0:T(8,128)(2,1)S(1)}, bf16[528,2048]{1,0:T(8,128)(2,1)S(1)}, u32[]{:S(2)}, u32[]{:S(2)}) collective-permute-start(bf16[528,2048]{1,0:T(8,128)(2,1)S(1)} %get-tuple-element.32.sketch_ref), channel_id=1, source_target_pairs={{1,0},{0,1},{3,2},{2,3},{5,4},{4,5},{7,6},{6,7},{9,8},{8,9},{11,10... | collective-permute-start | bytes 6488072 | tf_op jit(solution)/shard_map/ppermute | solution.py:338
  4.3 2.7 %collective-permute-start.2 = (bf16[512,2048]{1,0:T(8,128)(2,1)}, bf16[512,2048]{1,0:T(8,128)(2,1)S(1)}, u32[]{:S(2)}, u32[]{:S(2)}) collective-permute-start(bf16[512,2048]{1,0:T(8,128)(2,1)} %sketch_hbm.1), channel_id=1, source_target_pairs={{128,0},{385,1},{130,2},{387,3},{132,4},{389,5},{134,6},{391,7},{1... | collective-permute-start | bytes 6291464 | tf_op jit(solution)/shard_map/ppermute | solution.py:338
  7.1 13.3 %collective-permute-start.1 = (bf16[512,2048]{1,0:T(8,128)(2,1)}, bf16[512,2048]{1,0:T(8,128)(2,1)S(1)}, u32[]{:S(2)}, u32[]{:S(2)}) collective-permute-start(bf16[512,2048]{1,0:T(8,128)(2,1)} %sketch_hbm.1), channel_id=1, source_target_pairs={{127,0},{2,1},{1,2},{4,3},{3,4},{6,5},{5,6},{8,7},{7,8},{10,9},{9,... | collective-permute-start | bytes 6291464 | tf_op jit(solution)/shard_map/ppermute | solution.py:338
  20.4 3.4 %collective-permute-start.3 = (f32[1,2048]{1,0:T(1,128)S(1)}, f32[1,2048]{1,0:T(1,128)S(1)}, u32[]{:S(2)}, u32[]{:S(2)}) collective-permute-start(f32[1,2048]{1,0:T(1,128)S(1)} %get-tuple-element.35), channel_id=1, source_target_pairs={{384,0},{129,1},{386,2},{131,3},{388,4},{133,5},{390,6},{135,7},{3... | collective-permute-start | bytes 24584 | tf_op jit(solution)/shard_map/ppermute | solution.py:338
  23.8 0.0 collective-permute-done.mate_ref
  23.8 0.4 shard_map.51.d_ref
  24.2 1.9 %collective-permute-start.5 = (f32[1,2048]{1,0:T(1,128)S(1)}, f32[1,2048]{1,0:T(1,128)S(1)}, u32[]{:S(2)}, u32[]{:S(2)}) collective-permute-start(f32[1,2048]{1,0:T(1,128)S(1)} %shard_map.51.d_ref), channel_id=1, source_target_pairs={{510,0},{3,1},{0,2},{5,3},{2,4},{7,5},{4,6},{9,7},{6,8},{11,9},{8,... | collective-permute-start | bytes 24584 | tf_op jit(solution)/shard_map/ppermute | solution.py:338
  26.1 4.1 %collective-permute-start.4 = (f32[1,2048]{1,0:T(1,128)S(1)}, f32[1,2048]{1,0:T(1,128)S(1)}, u32[]{:S(2)}, u32[]{:S(2)}) collective-permute-start(f32[1,2048]{1,0:T(1,128)S(1)} %shard_map.51.d_ref), channel_id=1, source_target_pairs={{129,0},{384,1},{131,2},{386,3},{133,4},{388,5},{135,6},{390,7},{1... | collective-permute-start | bytes 24584 | tf_op jit(solution)/shard_map/ppermute | solution.py:338
  30.2 2.1 %shard_map.50 = (bf16[512,2560]{1,0:T(8,128)(2,1)}, f32[1,512]{1,0:T(1,128)S(1)}) custom-call(bf16[528,2048]{1,0:T(8,128)(2,1)S(1)} %get-tuple-element.32.sketch_ref, f32[8,512]{1,0:T(8,128)S(1)} %get-tuple-element.33.basis_ref), custom_call_target="tpu_custom_call" | custom-call | flops 1073741824 | bytes 2097152 | tf_op jit(solution)/shard_map/pallas_call | solution.py:116
  32.3 0.0 collective-permute-done.3.a_ref
  32.3 1.8 %collective-permute-done.5.c_ref = f32[1,2048]{1,0:T(1,128)S(1)} collective-permute-done((f32[1,2048]{1,0:T(1,128)S(1)}, f32[1,2048]{1,0:T(1,128)S(1)}, u32[]{:S(2)}, u32[]{:S(2)}) %collective-permute-start.5) | collective-permute-done | bytes 8224 | tf_op jit(solution)/shard_map/ppermute | solution.py:338
  34.1 0.0 collective-permute-done.4.b_ref
  34.1 1.2 %shard_map.52 = (f32[1,512]{1,0:T(1,128)S(1)}, f32[16,128]{1,0:T(8,128)S(1)}) custom-call(bf16[528,2048]{1,0:T(8,128)(2,1)S(1)} %get-tuple-element.32.sketch_ref, f32[8,512]{1,0:T(8,128)S(1)} %get-tuple-element.33.basis_ref, f32[1,512]{1,0:T(1,128)S(1)} %get-tuple-element.34.own_ref, f32[1,2048]{1,0:T(1,128)S(1)} %collective-permute-done.3.a_ref, ...), custom_call_target="tpu_custom_call" | custom-call | flops 33554432 | bytes 2097152 | tf_op jit(solution)/shard_map/pallas_call | solution.py:157
  35.3 10.1 %all_to_all.22 = f32[16,1,128]{2,1,0:T(1,128)S(1)} all-to-all(f32[16,1,128]{2,1,0:T(1,128)S(1)} %bitcast.19), channel_id=1, replica_groups=mesh['x'=4,'z'=8,'y'=8,'core'=2] {'z','core'}, dimensions={0} | all-to-all | bytes 16384 | tf_op jit(solution)/shard_map/all_to_all | solution.py:341
  45.5 0.0 collective-permute-done.2.far_ref
  45.5 0.0 collective-permute-done.1.near_ref
  45.5 1.3 %shard_map.54.token_ref = bf16[512,512]{1,0:T(8,128)(2,1)S(1)} custom-call(bf16[512,2048]{1,0:T(8,128)(2,1)S(1)} %collective-permute-done.2.far_ref, bf16[512,2048]{1,0:T(8,128)(2,1)S(1)} %collective-permute-done.1.near_ref, f32[32,128]{1,0:T(8,128)S(1)} %shard_map.53.token_ref), custom_call_target="tpu_custom_call" | custom-call | tf_op jit(solution)/shard_map/pallas_call | solution.py:202
  46.8 1.4 %shard_map.55 = (bf16[512,512]{1,0:T(8,128)(2,1)S(1)}, bf16[512,512]{1,0:T(8,128)(2,1)S(1)}) custom-call(bf16[528,2048]{1,0:T(8,128)(2,1)S(1)} %get-tuple-element.32.sketch_ref, bf16[512,2048]{1,0:T(8,128)(2,1)S(1)} %collective-permute-done.2.far_ref, bf16[512,512]{1,0:T(8,128)(2,1)S(1)} %shard_map.54.token_ref), custom_call_target="tpu_custom_call" | custom-call | flops 1073741824 | bytes 4194304 | tf_op jit(solution)/shard_map/pallas_call | solution.py:222
  48.1 4.6 %collective-permute-start.6 = (bf16[512,512]{1,0:T(8,128)(2,1)S(1)}, bf16[512,512]{1,0:T(8,128)(2,1)S(1)}, u32[]{:S(2)}, u32[]{:S(2)}) collective-permute-start(bf16[512,512]{1,0:T(8,128)(2,1)S(1)} %get-tuple-element.38), channel_id=1, source_target_pairs={{0,128},{1,385},{2,130},{3,387},{4,132},{5,389},{6,134},{7,391},{8... | collective-permute-start | bytes 1572872 | tf_op jit(solution)/shard_map/ppermute | solution.py:370
  52.7 1.9 %collective-permute-start.7 = (bf16[512,512]{1,0:T(8,128)(2,1)S(1)}, bf16[512,512]{1,0:T(8,128)(2,1)S(1)}, u32[]{:S(2)}, u32[]{:S(2)}) collective-permute-start(bf16[512,512]{1,0:T(8,128)(2,1)S(1)} %shard_map.54.token_ref), channel_id=1, source_target_pairs={{0,128},{127,511},{128,256},{255,127},{256,384},{383,255},{384,0},... | collective-permute-start | bytes 1572872 | tf_op jit(solution)/shard_map/ppermute | solution.py:369
  54.6 13.9 %all_to_all.23 = f32[32,1,128]{2,1,0:T(1,128)S(1)} all-to-all(f32[32,1,128]{2,1,0:T(1,128)S(1)} %bitcast.17), channel_id=1, replica_groups=mesh['x'=4,'z'=8,'y'=8,'core'=2] {'x','y'}, dimensions={0} | all-to-all | bytes 32768 | tf_op jit(solution)/shard_map/all_to_all | solution.py:341
  68.5 0.0 collective-permute-done.6.back_ref
  68.5 0.0 collective-permute-done.7.corner_ref
  68.5 3.4 %shard_map.56 = (bf16[512,2560]{1,0:T(8,128)(2,1)}, f32[8,128]{1,0:T(8,128)S(1)}) custom-call(bf16[528,2048]{1,0:T(8,128)(2,1)S(1)} %get-tuple-element.32.sketch_ref, bf16[528,2048]{1,0:T(8,128)(2,1)S(1)} %collective-permute-done.mate_ref, bf16[512,2048]{1,0:T(8,128)(2,1)S(1)} %collective-permute-done.1.near_ref, ...), custom_call_target="tpu_custom_call", output_to_operand_aliasing={{0}: (7, {})} | custom-call | flops 2147483648 | bytes 4194304 | tf_op jit(solution)/shard_map/pallas_call | solution.py:272
  71.9 0.7 shard_map.57
  73.3 0.0 copy-start
  73.3 0.0 copy-start.1
  73.4 0.6 copy-done
  73.9 0.0 copy-done.1
  (3 shorter events, 0.0 us)
Async XLA Ops:
  2.4 21.4 %collective-permute-start = (bf16[528,2048]{1,0:T(8,128)(2,1)S(1)}, bf16[528,2048]{1,0:T(8,128)(2,1)S(1)}, u32[]{:S(2)}, u32[]{:S(2)}) collective-permute-start(bf16[528,2048]{1,0:T(8,128)(2,1)S(1)} %get-tuple-element.32.sketch_ref), channel_id=1, source_target_pairs={{1,0},{0,1},{3,2},{2,3},{5,4},{4,5},{7,6},{6,7},{9,8},{8,9},{11,10... | collective-permute-start | bytes 6488072 | tf_op jit(solution)/shard_map/ppermute | solution.py:338
  4.3 41.1 %collective-permute-start.2 = (bf16[512,2048]{1,0:T(8,128)(2,1)}, bf16[512,2048]{1,0:T(8,128)(2,1)S(1)}, u32[]{:S(2)}, u32[]{:S(2)}) collective-permute-start(bf16[512,2048]{1,0:T(8,128)(2,1)} %sketch_hbm.1), channel_id=1, source_target_pairs={{128,0},{385,1},{130,2},{387,3},{132,4},{389,5},{134,6},{391,7},{1... | collective-permute-start | bytes 6291464 | tf_op jit(solution)/shard_map/ppermute | solution.py:338
  7.1 38.4 %collective-permute-start.1 = (bf16[512,2048]{1,0:T(8,128)(2,1)}, bf16[512,2048]{1,0:T(8,128)(2,1)S(1)}, u32[]{:S(2)}, u32[]{:S(2)}) collective-permute-start(bf16[512,2048]{1,0:T(8,128)(2,1)} %sketch_hbm.1), channel_id=1, source_target_pairs={{127,0},{2,1},{1,2},{4,3},{3,4},{6,5},{5,6},{8,7},{7,8},{10,9},{9,... | collective-permute-start | bytes 6291464 | tf_op jit(solution)/shard_map/ppermute | solution.py:338
  20.4 11.9 %collective-permute-start.3 = (f32[1,2048]{1,0:T(1,128)S(1)}, f32[1,2048]{1,0:T(1,128)S(1)}, u32[]{:S(2)}, u32[]{:S(2)}) collective-permute-start(f32[1,2048]{1,0:T(1,128)S(1)} %get-tuple-element.35), channel_id=1, source_target_pairs={{384,0},{129,1},{386,2},{131,3},{388,4},{133,5},{390,6},{135,7},{3... | collective-permute-start | bytes 24584 | tf_op jit(solution)/shard_map/ppermute | solution.py:338
  24.2 9.9 %collective-permute-start.5 = (f32[1,2048]{1,0:T(1,128)S(1)}, f32[1,2048]{1,0:T(1,128)S(1)}, u32[]{:S(2)}, u32[]{:S(2)}) collective-permute-start(f32[1,2048]{1,0:T(1,128)S(1)} %shard_map.51.d_ref), channel_id=1, source_target_pairs={{510,0},{3,1},{0,2},{5,3},{2,4},{7,5},{4,6},{9,7},{6,8},{11,9},{8,... | collective-permute-start | bytes 24584 | tf_op jit(solution)/shard_map/ppermute | solution.py:338
  26.1 8.0 %collective-permute-start.4 = (f32[1,2048]{1,0:T(1,128)S(1)}, f32[1,2048]{1,0:T(1,128)S(1)}, u32[]{:S(2)}, u32[]{:S(2)}) collective-permute-start(f32[1,2048]{1,0:T(1,128)S(1)} %shard_map.51.d_ref), channel_id=1, source_target_pairs={{129,0},{384,1},{131,2},{386,3},{133,4},{388,5},{135,6},{390,7},{1... | collective-permute-start | bytes 24584 | tf_op jit(solution)/shard_map/ppermute | solution.py:338
  48.1 20.4 %collective-permute-start.6 = (bf16[512,512]{1,0:T(8,128)(2,1)S(1)}, bf16[512,512]{1,0:T(8,128)(2,1)S(1)}, u32[]{:S(2)}, u32[]{:S(2)}) collective-permute-start(bf16[512,512]{1,0:T(8,128)(2,1)S(1)} %get-tuple-element.38), channel_id=1, source_target_pairs={{0,128},{1,385},{2,130},{3,387},{4,132},{5,389},{6,134},{7,391},{8... | collective-permute-start | bytes 1572872 | tf_op jit(solution)/shard_map/ppermute | solution.py:370
  52.7 15.8 %collective-permute-start.7 = (bf16[512,512]{1,0:T(8,128)(2,1)S(1)}, bf16[512,512]{1,0:T(8,128)(2,1)S(1)}, u32[]{:S(2)}, u32[]{:S(2)}) collective-permute-start(bf16[512,512]{1,0:T(8,128)(2,1)S(1)} %shard_map.54.token_ref), channel_id=1, source_target_pairs={{0,128},{127,511},{128,256},{255,127},{256,384},{383,255},{384,0},... | collective-permute-start | bytes 1572872 | tf_op jit(solution)/shard_map/ppermute | solution.py:369
  73.3 0.6 copy-start
  73.3 0.6 copy-start.1

commit v4 on v3

--- a/solution.py
+++ b/solution.py
@@ -98,32 +98,47 @@
     )(mate)
 
 
-def own_block_kernel(sketch_ref, basis_ref, rows_ref, own_image_ref, block_ref, sem):
+def column_copy(block_ref, rows_ref, column, sem):
+    n = block_ref.shape[0]
+    start = column * n if isinstance(column, int) else pl.multiple_of(column * n, n)
+    return pltpu.make_async_copy(block_ref, rows_ref.at[:, pl.ds(start, n)], sem)
+
+
+def plane_rank():
+    rank, size = 0, 1
+    for name in AXES[1:]:
+        rank = rank * lax.axis_size(name) + lax.axis_index(name)
+        size = size * lax.axis_size(name)
+    return rank, size - 1
+
+
+def own_blocks_kernel(sketch_ref, mate_ref, basis_ref, rows_ref, own_image_ref, mate_block_ref, block_ref, sem):
     last = basis_ref.shape[0] - 1
     n = block_ref.shape[0]
     current = basis_ref[last : last + 1, :].astype(BF16)
     sketch = sketch_ref[:n, :]
     block = dot_last(sketch, sketch).astype(BF16)
     block_ref[...] = block
-    copy = pltpu.make_async_copy(block_ref, rows_ref.at[:, pl.ds(0, n)], sem)
+    copy = column_copy(block_ref, rows_ref, 0, sem)
     copy.start()
     own_image_ref[...] = dot_last(jnp.broadcast_to(current, (16, n)), block)[0:1, :]
+    mate_block_ref[...] = dot_last(sketch, mate_ref[:n, :]).astype(BF16)
     copy.wait()
 
 
-def own_block(sketch, basis):
+def own_blocks(sketch, mate, basis):
     n, k = basis.shape[1], sketch.shape[1]
     return pl.pallas_call(
-        own_block_kernel,
-        out_shape=(shaped((n, BANDS * n), BF16), shaped((1, n))),
-        in_specs=[whole(), whole()],
-        out_specs=(whole(pl.ANY), whole()),
+        own_blocks_kernel,
+        out_shape=(shaped((n, BANDS * n), BF16), shaped((1, n)), shaped((n, n), BF16)),
+        in_specs=[whole()] * 3,
+        out_specs=(whole(pl.ANY), whole(), whole()),
         scratch_shapes=[pltpu.VMEM((n, n), BF16), pltpu.SemaphoreType.DMA],
         compiler_params=params(),
         cost_estimate=pl.CostEstimate(
-            flops=2 * n * n * k, bytes_accessed=2 * n * k, transcendentals=0
+            flops=4 * n * n * k, bytes_accessed=2 * n * k, transcendentals=0
         ),
-    )(sketch, basis)
+    )(sketch, mate, basis)
 
 
 def image_kernel(sketch_ref, basis_ref, own_ref, a_ref, b_ref, c_ref, d_ref, image_ref, sums_ref):
@@ -181,106 +196,116 @@
     )(rows)
 
 
-def plane_rank():
-    rank, size = 0, 1
-    for name in AXES[1:]:
-        rank = rank * lax.axis_size(name) + lax.axis_index(name)
-        size = size * lax.axis_size(name)
-    return rank, size - 1
-
-
-def corner_kernel(far_ref, near_ref, token_ref, corner_ref):
-    del token_ref
+def near_kernel(
+    sketch_ref, far_ref, near_ref, mate_block_ref, token_ref, rows_in_ref, rows_ref, block_ref, sem
+):
+    del token_ref, rows_in_ref
+    copy = column_copy(mate_block_ref, rows_ref, 1 + lax.axis_index("core"), sem)
+    copy.start()
     rank, last = plane_rank()
-
-    @pl.when((rank == 0) | (rank == last))
+    is_corner = (rank == 0) | (rank == last)
+
+    @pl.when(is_corner)
     def _():
-        corner_ref[...] = dot_last(far_ref[...], near_ref[...]).astype(BF16)
-
-
-def corner_block(far, near, token, n):
-    return pl.pallas_call(
-        corner_kernel,
-        out_shape=shaped((n, n), BF16),
-        in_specs=[whole()] * 3,
-        out_specs=whole(),
-        compiler_params=params(),
-    )(far, near, token)
-
-
-def far_kernel(sketch_ref, far_ref, token_ref, back_ref, block_ref):
-    del token_ref
-    n = back_ref.shape[0]
-    back = dot_last(far_ref[...], sketch_ref[:n, :]).astype(BF16)
-    back_ref[...] = back
-    block_ref[...] = back.T
-
-
-def far_blocks(sketch, far, token, n):
-    k = sketch.shape[1]
-    block = shaped((n, n), BF16)
-    return pl.pallas_call(
-        far_kernel,
-        out_shape=(block, block),
-        in_specs=[whole()] * 3,
-        out_specs=(whole(), whole()),
+        block_ref[...] = dot_last(far_ref[...], near_ref[...]).astype(BF16)
+
+    @pl.when(jnp.logical_not(is_corner))
+    def _():
+        block_ref[...] = dot_last(sketch_ref[: block_ref.shape[0], :], near_ref[...]).astype(BF16)
+
+    copy.wait()
+
+
+def near_block(sketch, far, near, mate_block, token, rows):
+    n, k = near.shape
+    return pl.pallas_call(
+        near_kernel,
+        out_shape=(shaped(rows.shape, rows.dtype), shaped((n, n), BF16)),
+        in_specs=[whole()] * 5 + [whole(pl.ANY)],
+        out_specs=(whole(pl.ANY), whole()),
+        scratch_shapes=[pltpu.SemaphoreType.DMA],
+        input_output_aliases={5: 0},
         compiler_params=params(),
         cost_estimate=pl.CostEstimate(
             flops=2 * n * n * k, bytes_accessed=4 * n * k, transcendentals=0
         ),
-    )(sketch, far, token)
-
-
-def column_copy(block_ref, rows_ref, column, sem):
-    n = block_ref.shape[0]
-    start = column * n if isinstance(column, int) else pl.multiple_of(column * n, n)
-    return pltpu.make_async_copy(block_ref, rows_ref.at[:, pl.ds(start, n)], sem)
-
-
-def pairs_kernel(
-    sketch_ref, mate_ref, near_ref, far_ref, back_ref, corner_ref, sums_ref, rows_in_ref,
-    rows_ref, token_ref, blocks_ref, sems,
-):
-    del sums_ref, rows_in_ref
-    token_ref[...] = jnp.zeros_like(token_ref)
-    n = far_ref.shape[0]
-    core = lax.axis_index("core")
+    )(sketch, far, near, mate_block, token, rows)
+
+
+def far_kernel(sketch_ref, far_ref, near_block_ref, rows_in_ref, rows_ref, back_ref, block_ref, sem):
+    del rows_in_ref
+    copy = column_copy(near_block_ref, rows_ref, 2 - lax.axis_index("core"), sem)
+    copy.start()
+    back = dot_last(far_ref[...], sketch_ref[: back_ref.shape[0], :]).astype(BF16)
+    back_ref[...] = back
+    block_ref[...] = back.T
+    copy.wait()
+
+
+def far_blocks(sketch, far, near_block, rows):
+    n, k = far.shape
+    block = shaped((n, n), BF16)
+    return pl.pallas_call(
+        far_kernel,
+        out_shape=(shaped(rows.shape, rows.dtype), block, block),
+        in_specs=[whole()] * 3 + [whole(pl.ANY)],
+        out_specs=(whole(pl.ANY), whole(), whole()),
+        scratch_shapes=[pltpu.SemaphoreType.DMA],
+        input_output_aliases={3: 0},
+        compiler_params=params(),
+        cost_estimate=pl.CostEstimate(
+            flops=2 * n * n * k, bytes_accessed=4 * n * k, transcendentals=0
+        ),
+    )(sketch, far, near_block, rows)
+
+
+def place_corner_kernel(corner_ref, rows_in_ref, rows_ref, sem):
+    del rows_in_ref
     rank, last = plane_rank()
-    copies = [
-        column_copy(far_ref, rows_ref, 3 + core, sems.at[0]),
-        column_copy(back_ref, rows_ref, 4 - core, sems.at[1]),
-    ]
-    for copy in copies:
-        copy.start()
-    blocks_ref[0] = dot_last(sketch_ref[:n, :], mate_ref[:n, :]).astype(BF16)
-    copies.append(column_copy(blocks_ref.at[0], rows_ref, 1 + core, sems.at[2]))
-    copies[-1].start()
-    blocks_ref[1] = dot_last(sketch_ref[:n, :], near_ref[...]).astype(BF16)
 
     @pl.when((rank == 0) | (rank == last))
     def _():
-        blocks_ref[1] = corner_ref[...]
-
-    copies.append(column_copy(blocks_ref.at[1], rows_ref, 2 - core, sems.at[3]))
-    copies[-1].start()
-    for copy in copies:
+        copy = column_copy(corner_ref, rows_ref, 2 - lax.axis_index("core"), sem)
+        copy.start()
         copy.wait()
 
 
-def pair_blocks(sketch, mate, near, far, back, corner, sums, rows):
-    n, k = near.shape
-    return pl.pallas_call(
-        pairs_kernel,
+def place_corner(corner, rows):
+    return pl.pallas_call(
+        place_corner_kernel,
+        out_shape=shaped(rows.shape, rows.dtype),
+        in_specs=[whole(), whole(pl.ANY)],
+        out_specs=whole(pl.ANY),
+        scratch_shapes=[pltpu.SemaphoreType.DMA],
+        input_output_aliases={1: 0},
+        compiler_params=params(),
+        cost_estimate=pl.CostEstimate(flops=0, bytes_accessed=2 * corner.size, transcendentals=0),
+    )(corner, rows)
+
+
+def place_far_kernel(far_ref, back_ref, rows_in_ref, rows_ref, token_ref, sems):
+    del rows_in_ref
+    token_ref[...] = jnp.zeros_like(token_ref)
+    core = lax.axis_index("core")
+    far = column_copy(far_ref, rows_ref, 3 + core, sems.at[0])
+    back = column_copy(back_ref, rows_ref, 4 - core, sems.at[1])
+    far.start()
+    back.start()
+    far.wait()
+    back.wait()
+
+
+def place_far(far, back, rows):
+    return pl.pallas_call(
+        place_far_kernel,
         out_shape=(shaped(rows.shape, rows.dtype), shaped((8, 128))),
-        in_specs=[whole()] * 7 + [whole(pl.ANY)],
+        in_specs=[whole()] * 2 + [whole(pl.ANY)],
         out_specs=(whole(pl.ANY), whole()),
-        scratch_shapes=[pltpu.VMEM((2, n, n), BF16), pltpu.SemaphoreType.DMA((4,))],
-        input_output_aliases={7: 0},
-        compiler_params=params(),
-        cost_estimate=pl.CostEstimate(
-            flops=4 * n * n * k, bytes_accessed=4 * n * k, transcendentals=0
-        ),
-    )(sketch, mate, near, far, back, corner, sums, rows)
+        scratch_shapes=[pltpu.SemaphoreType.DMA((2,))],
+        input_output_aliases={2: 0},
+        compiler_params=params(),
+        cost_estimate=pl.CostEstimate(flops=0, bytes_accessed=8 * far.size, transcendentals=0),
+    )(far, back, rows)
 
 
 def finish_kernel(count, sums_ref, basis_ref, image_ref, token_ref, left_ref, next_ref, stats_ref, lost_ref):
@@ -340,8 +365,6 @@
     def trade(rows, group):
         return lax.all_to_all(rows, group, 0, 0, tiled=True)
 
-    rows_each = sketch.shape[0]
-
     def in_plane(i, step):
         return i // stride * stride + (i + step) % stride
 
@@ -357,19 +380,20 @@
         move(mate_u, lambda i: i - 2 if i % 2 == 0 else i + 2),
         mate_u,
     )
-    rows, own_image = own_block(sketch, basis)
+    rows, own_image, mate_block = own_blocks(sketch, mate, basis)
     image, sums = image_and_sums(sketch, basis, own_image, parts, group_size(FIRST_GROUP))
     sums = add_and_copy(trade(sums, FIRST_GROUP), group_size(SECOND_GROUP))
-    corner = corner_block(far, near, sums, rows_each)
-    far_back, far_block = far_blocks(sketch, far, corner, rows_each)
+    rows, near = near_block(sketch, far, near, mate_block, sums, rows)
+    rows, far_back, far_block = far_blocks(sketch, far, near, rows)
     def to_sender(i):
         return (i + stride if i % 2 == 0 else i - stride) % devices
 
     corners = [i for i in range(devices) if i % stride in (0, stride - 1)]
-    corner = lax.ppermute(corner, AXES, [(i, to_sender(i)) for i in corners] + [(2, 4)])
+    corner = lax.ppermute(near, AXES, [(i, to_sender(i)) for i in corners] + [(2, 4)])
     far_back = lax.ppermute(far_back, AXES, [(i, to_sender(i)) for i in range(devices)])
     sums = trade(sums, SECOND_GROUP)
-    rows, token = pair_blocks(sketch, mate, near, far_block, far_back, corner, sums, rows)
+    rows = place_corner(corner, rows)
+    rows, token = place_far(far_block, far_back, rows)
     left, next_vector, stats, lost = finish(sums, basis, image, float(total_rows), token)
 
     m = basis.shape[0]

time: 75.1 us -> 73.8 us (0.983)
  blocking collectives: 24 us -> 10.1 us
  waiting for transfers between devices: 1.82 us -> 9.03 us
  starting transfers between devices: 33.9 us -> 38.5 us
    all_to_all x2 -> x1, blocking collectives: 24 us -> 10.1 us  [trade(): return lax.all_to_all(rows, group, 0, 0, tiled=True)]
    all_to_all x0 -> x1, starting transfers between devices: none -> 6.17 us  [trade(): return lax.all_to_all(rows, group, 0, 0, tiled=True)]
    ppermute x1, waiting for transfers between devices: 0.01 us -> 3.06 us  [on_device(): lax.ppermute(far_back, AXES, [(i, to_sender(i)) for i in range(devices)])]
    all_to_all x0 -> x1, waiting for transfers between devices: none -> 3.01 us  [trade(): return lax.all_to_all(rows, group, 0, 0, tiled=True)]
    ppermute x1, starting transfers between devices: 4.58 us -> 1.92 us  [on_device(): lax.ppermute(far_back, AXES, [(i, to_sender(i)) for i in range(devices)])]
    ppermute x6, waiting for transfers between devices: 1.81 us -> 2.95 us  [move(): lax.ppermute(block, AXES, [(source_of(i) % devices, i) for i in range(dev...]
    ppermute x1, starting transfers between devices: 1.92 us -> 3 us  [on_device(): lax.ppermute(near, AXES, [(i, to_sender(i)) for i in corners] + [(2, 4)])]
    pallas_call x4 -> x5, Pallas kernels: 8.11 us -> 8.21 us  [the longest x1 2.63 us: own_blocks(): pl.pallas_call(own_blocks_kernel, out_shape=(shaped((n, BANDS * n), BF16)...]
  transfers between devices with their start and end apart: 8 -> 9, of which waited for: 1 -> 4; matrix products, arithmetic and copies ran while one was open for 0% -> 0% of each run, Pallas kernels for 5% -> 12%
where the time goes in v4:
time: 73.8 us; the launch traced here: 72.5 us
  starting transfers between devices  38.5 us (52%)
  Pallas kernels  12.9 us (17%)
  blocking collectives  10.1 us (14%)
  waiting for transfers between devices  9.03 us (12%)
  between operations  1.46 us (2%)
    ppermute x6, starting transfers between devices, move(): lax.ppermute(block, AXES, [(source_of(i) % devices, i) for i in range(dev...  27.4 us
    all_to_all x1, blocking collectives, trade(): return lax.all_to_all(rows, group, 0, 0, tiled=True)  10.1 us
    all_to_all x1, starting transfers between devices, trade(): return lax.all_to_all(rows, group, 0, 0, tiled=True)  6.17 us
    ppermute x1, waiting for transfers between devices, on_device(): lax.ppermute(far_back, AXES, [(i, to_sender(i)) for i in range(devices)])  3.06 us
    all_to_all x1, waiting for transfers between devices, trade(): return lax.all_to_all(rows, group, 0, 0, tiled=True)  3.01 us
    ppermute x1, starting transfers between devices, on_device(): lax.ppermute(near, AXES, [(i, to_sender(i)) for i in corners] + [(2, 4)])  3 us
    ppermute x6, waiting for transfers between devices, move(): lax.ppermute(block, AXES, [(source_of(i) % devices, i) for i in range(dev...  2.95 us
    pallas_call x1, Pallas kernels, own_blocks(): pl.pallas_call(own_blocks_kernel, out_shape=(shaped((n, BANDS * n), BF16)...  2.63 us
  transfers between devices with their start and end apart: 9, of which 4 were waited for; matrix products, arithmetic and copies ran while one was open for 0% of the time, Pallas kernels for 12%

profile of v4, /device:TPU:6, one launch (start us, length us, event | category | flops | bytes accessed | tf_op | source)
XLA Modules:
  0.0 72.5 jit_solution(6974664794099091316)
XLA Ops:
  0.6 1.8 %shard_map.49 = (bf16[528,2048]{1,0:T(8,128)(2,1)S(1)}, f32[1,2048]{1,0:T(1,128)S(1)}, f32[8,512]{1,0:T(8,128)S(1)}) custom-call(bf16[512,2048]{1,0:T(8,128)(2,1)} %sketch_hbm.1, f32[8,512]{1,0:T(8,128)} %basis_hbm.1), custom_call_target="tpu_custom_call" | custom-call | flops 2097152 | tf_op jit(solution)/shard_map/pallas_call | solution.py:71
  2.4 1.9 %collective-permute-start.2 = (bf16[528,2048]{1,0:T(8,128)(2,1)S(1)}, bf16[528,2048]{1,0:T(8,128)(2,1)S(1)}, u32[]{:S(2)}, u32[]{:S(2)}) collective-permute-start(bf16[528,2048]{1,0:T(8,128)(2,1)S(1)} %get-tuple-element.36.sketch_ref), channel_id=1, source_target_pairs={{1,0},{0,1},{3,2},{2,3},{5,4},{4,5},{7,6},{6,7},{9,8},{8,9},{11,10... | collective-permute-start | bytes 6488072 | tf_op jit(solution)/shard_map/ppermute | solution.py:363
  4.3 14.0 %collective-permute-start.1 = (bf16[512,2048]{1,0:T(8,128)(2,1)}, bf16[512,2048]{1,0:T(8,128)(2,1)S(1)}, u32[]{:S(2)}, u32[]{:S(2)}) collective-permute-start(bf16[512,2048]{1,0:T(8,128)(2,1)} %sketch_hbm.1), channel_id=1, source_target_pairs={{127,0},{2,1},{1,2},{4,3},{3,4},{6,5},{5,6},{8,7},{7,8},{10,9},{9,... | collective-permute-start | bytes 6291464 | tf_op jit(solution)/shard_map/ppermute | solution.py:363
  18.3 2.7 %collective-permute-start = (bf16[512,2048]{1,0:T(8,128)(2,1)}, bf16[512,2048]{1,0:T(8,128)(2,1)S(1)}, u32[]{:S(2)}, u32[]{:S(2)}) collective-permute-start(bf16[512,2048]{1,0:T(8,128)(2,1)} %sketch_hbm.1), channel_id=1, source_target_pairs={{128,0},{385,1},{130,2},{387,3},{132,4},{389,5},{134,6},{391,7},{1... | collective-permute-start | bytes 6291464 | tf_op jit(solution)/shard_map/ppermute | solution.py:363
  21.0 4.3 %collective-permute-start.3 = (f32[1,2048]{1,0:T(1,128)S(1)}, f32[1,2048]{1,0:T(1,128)S(1)}, u32[]{:S(2)}, u32[]{:S(2)}) collective-permute-start(f32[1,2048]{1,0:T(1,128)S(1)} %get-tuple-element.40), channel_id=1, source_target_pairs={{384,0},{129,1},{386,2},{131,3},{388,4},{133,5},{390,6},{135,7},{3... | collective-permute-start | bytes 24584 | tf_op jit(solution)/shard_map/ppermute | solution.py:363
  25.4 0.0 collective-permute-done.2.mate_ref
  25.4 0.4 shard_map.51.d_ref
  25.8 1.9 %collective-permute-start.5 = (f32[1,2048]{1,0:T(1,128)S(1)}, f32[1,2048]{1,0:T(1,128)S(1)}, u32[]{:S(2)}, u32[]{:S(2)}) collective-permute-start(f32[1,2048]{1,0:T(1,128)S(1)} %shard_map.51.d_ref), channel_id=1, source_target_pairs={{510,0},{3,1},{0,2},{5,3},{2,4},{7,5},{4,6},{9,7},{6,8},{11,9},{8,... | collective-permute-start | bytes 24584 | tf_op jit(solution)/shard_map/ppermute | solution.py:363
  27.7 2.5 %collective-permute-start.4 = (f32[1,2048]{1,0:T(1,128)S(1)}, f32[1,2048]{1,0:T(1,128)S(1)}, u32[]{:S(2)}, u32[]{:S(2)}) collective-permute-start(f32[1,2048]{1,0:T(1,128)S(1)} %shard_map.51.d_ref), channel_id=1, source_target_pairs={{129,0},{384,1},{131,2},{386,3},{133,4},{388,5},{135,6},{390,7},{1... | collective-permute-start | bytes 24584 | tf_op jit(solution)/shard_map/ppermute | solution.py:363
  30.2 2.6 %shard_map.50 = (bf16[512,2560]{1,0:T(8,128)(2,1)}, f32[1,512]{1,0:T(1,128)S(1)}, bf16[512,512]{1,0:T(8,128)(2,1)S(1)}) custom-call(bf16[528,2048]{1,0:T(8,128)(2,1)S(1)} %get-tuple-element.36.sketch_ref, bf16[528,2048]{1,0:T(8,128)(2,1)S(1)} %collective-permute-done.2.mate_ref, f32[8,512]{1,0:T(8,128)S(1)} %get-tuple-element.37.basis_ref), custom_call_target="tpu_custom_call" | custom-call | flops 2147483648 | bytes 2097152 | tf_op jit(solution)/shard_map/pallas_call | solution.py:131
  32.9 0.0 collective-permute-done.3.a_ref
  32.9 2.8 %collective-permute-done.5.c_ref = f32[1,2048]{1,0:T(1,128)S(1)} collective-permute-done((f32[1,2048]{1,0:T(1,128)S(1)}, f32[1,2048]{1,0:T(1,128)S(1)}, u32[]{:S(2)}, u32[]{:S(2)}) %collective-permute-start.5) | collective-permute-done | bytes 8224 | tf_op jit(solution)/shard_map/ppermute | solution.py:363
  35.7 0.0 collective-permute-done.4.b_ref
  35.7 1.2 %shard_map.52 = (f32[1,512]{1,0:T(1,128)S(1)}, f32[16,128]{1,0:T(8,128)S(1)}) custom-call(bf16[528,2048]{1,0:T(8,128)(2,1)S(1)} %get-tuple-element.36.sketch_ref, f32[8,512]{1,0:T(8,128)S(1)} %get-tuple-element.37.basis_ref, f32[1,512]{1,0:T(1,128)S(1)} %get-tuple-element.39.own_ref, f32[1,2048]{1,0:T(1,128)S(1)} %collective-permute-done.3.a_ref, ...), custom_call_target="tpu_custom_call" | custom-call | flops 33554432 | bytes 2097152 | tf_op jit(solution)/shard_map/pallas_call | solution.py:172
  36.9 10.1 %all_to_all.22 = f32[16,1,128]{2,1,0:T(1,128)S(1)} all-to-all(f32[16,1,128]{2,1,0:T(1,128)S(1)} %bitcast.17), channel_id=1, replica_groups=mesh['x'=4,'z'=8,'y'=8,'core'=2] {'z','core'}, dimensions={0} | all-to-all | bytes 16384 | tf_op jit(solution)/shard_map/all_to_all | solution.py:366
  47.0 0.6 shard_map.53.token_ref
  47.6 0.0 collective-permute-done.1.near_ref
  47.6 0.1 collective-permute-done.far_ref
  47.7 2.0 %shard_map.54 = (bf16[512,2560]{1,0:T(8,128)(2,1)}, bf16[512,512]{1,0:T(8,128)(2,1)S(1)}) custom-call(bf16[528,2048]{1,0:T(8,128)(2,1)S(1)} %get-tuple-element.36.sketch_ref, bf16[512,2048]{1,0:T(8,128)(2,1)S(1)} %collective-permute-done.far_ref, bf16[512,2048]{1,0:T(8,128)(2,1)S(1)} %collective-permute-done.1.near_ref, ...), custom_call_target="tpu_custom_call", output_to_operand_aliasing={{0}: (5, {})} | custom-call | flops 1073741824 | bytes 4194304 | tf_op jit(solution)/shard_map/pallas_call | solution.py:221
  49.8 3.0 %collective-permute-start.7 = (bf16[512,512]{1,0:T(8,128)(2,1)S(1)}, bf16[512,512]{1,0:T(8,128)(2,1)S(1)}, u32[]{:S(2)}, u32[]{:S(2)}) collective-permute-start(bf16[512,512]{1,0:T(8,128)(2,1)S(1)} %get-tuple-element.43.near_block_ref), channel_id=1, source_target_pairs={{0,128},{127,511},{128,256},{255,127},{256,384},{383,255},{384,0},... | collective-permute-start | bytes 1572872 | tf_op jit(solution)/shard_map/ppermute | solution.py:392
  52.8 1.8 %shard_map.55 = (bf16[512,2560]{1,0:T(8,128)(2,1)}, bf16[512,512]{1,0:T(8,128)(2,1)S(1)}, bf16[512,512]{1,0:T(8,128)(2,1)S(1)}) custom-call(bf16[528,2048]{1,0:T(8,128)(2,1)S(1)} %get-tuple-element.36.sketch_ref, bf16[512,2048]{1,0:T(8,128)(2,1)S(1)} %collective-permute-done.far_ref, ...), custom_call_target="tpu_custom_call", output_to_operand_aliasing={{0}: (3, {})} | custom-call | flops 1073741824 | bytes 4194304 | tf_op jit(solution)/shard_map/pallas_call | solution.py:248
  54.5 1.9 %collective-permute-start.6 = (bf16[512,512]{1,0:T(8,128)(2,1)S(1)}, bf16[512,512]{1,0:T(8,128)(2,1)S(1)}, u32[]{:S(2)}, u32[]{:S(2)}) collective-permute-start(bf16[512,512]{1,0:T(8,128)(2,1)S(1)} %get-tuple-element.46), channel_id=1, source_target_pairs={{0,128},{1,385},{2,130},{3,387},{4,132},{5,389},{6,134},{7,391},{8... | collective-permute-start | bytes 1572872 | tf_op jit(solution)/shard_map/ppermute | solution.py:393
  56.5 6.2 %all-to-all-start.1 = ((f32[32,1,128]{2,1,0:T(1,128)}), f32[32,1,128]{2,1,0:T(1,128)S(1)}, u32[]{:S(2)}, u32[]{:S(2)}) async-start(f32[32,1,128]{2,1,0:T(1,128)} %bitcast.7), calls=%async_computation.1 | async-start | bytes 32768 | tf_op jit(solution)/shard_map/all_to_all | solution.py:366
  62.6 0.0 collective-permute-done.7.corner_ref
  62.7 0.8 %shard_map.56.rows_in_ref = bf16[512,2560]{1,0:T(8,128)(2,1)} custom-call(bf16[512,512]{1,0:T(8,128)(2,1)S(1)} %collective-permute-done.7.corner_ref, bf16[512,2560]{1,0:T(8,128)(2,1)} %get-tuple-element.47.rows_in_ref), custom_call_target="tpu_custom_call", output_to_operand_aliasing={{}: (1, {})} | custom-call | bytes 524288 | tf_op jit(solution)/shard_map/pallas_call | solution.py:274
  63.5 3.1 %collective-permute-done.6.back_ref = bf16[512,512]{1,0:T(8,128)(2,1)S(1)} collective-permute-done((bf16[512,512]{1,0:T(8,128)(2,1)S(1)}, bf16[512,512]{1,0:T(8,128)(2,1)S(1)}, u32[]{:S(2)}, u32[]{:S(2)}) %collective-permute-start.6) | collective-permute-done | bytes 524320 | tf_op jit(solution)/shard_map/ppermute | solution.py:393
  66.5 1.0 %shard_map.57 = (bf16[512,2560]{1,0:T(8,128)(2,1)}, f32[8,128]{1,0:T(8,128)S(1)}) custom-call(bf16[512,512]{1,0:T(8,128)(2,1)S(1)} %get-tuple-element.45.far_ref, bf16[512,512]{1,0:T(8,128)(2,1)S(1)} %collective-permute-done.6.back_ref, bf16[512,2560]{1,0:T(8,128)(2,1)} %shard_map.56.rows_in_ref), custom_call_target="tpu_custom_call", output_to_operand_aliasing={{0}: (2, {})} | custom-call | bytes 2097152 | tf_op jit(solution)/shard_map/pallas_call | solution.py:299
  67.5 3.0 %all-to-all-done.1 = f32[32,1,128]{2,1,0:T(1,128)S(1)} async-done(((f32[32,1,128]{2,1,0:T(1,128)}), f32[32,1,128]{2,1,0:T(1,128)S(1)}, u32[]{:S(2)}, u32[]{:S(2)}) %all-to-all-start.1) | async-done | bytes 16416 | tf_op jit(solution)/shard_map/all_to_all | solution.py:366
  70.5 0.7 %shard_map.58 = (f32[1,512]{1,0:T(1,128)S(1)}, f32[1,512]{1,0:T(1,128)S(1)}, f32[1,128]{1,0:T(1,128)S(1)}, s32[1]{0:T(128)}) custom-call(f32[32,128]{1,0:T(8,128)S(1)} %bitcast.15, f32[8,512]{1,0:T(8,128)S(1)} %get-tuple-element.37.basis_ref, f32[1,512]{1,0:T(1,128)S(1)} %get-tuple-element.49.image_ref, f32[8,128]{1,0:T(8,128)S(1)} %get-tuple-element.50.token_ref), custom_call_target="tpu_custom_call" | custom-call | tf_op jit(solution)/shard_map/pallas_call | solution.py:341
  72.0 0.0 copy-start
  72.0 0.0 copy-start.1
  72.0 0.6 copy-done
  72.5 0.0 copy-done.1
  (2 shorter events, 0.0 us)
Async XLA Ops:
  2.4 23.0 %collective-permute-start.2 = (bf16[528,2048]{1,0:T(8,128)(2,1)S(1)}, bf16[528,2048]{1,0:T(8,128)(2,1)S(1)}, u32[]{:S(2)}, u32[]{:S(2)}) collective-permute-start(bf16[528,2048]{1,0:T(8,128)(2,1)S(1)} %get-tuple-element.36.sketch_ref), channel_id=1, source_target_pairs={{1,0},{0,1},{3,2},{2,3},{5,4},{4,5},{7,6},{6,7},{9,8},{8,9},{11,10... | collective-permute-start | bytes 6488072 | tf_op jit(solution)/shard_map/ppermute | solution.py:363
  4.3 43.3 %collective-permute-start.1 = (bf16[512,2048]{1,0:T(8,128)(2,1)}, bf16[512,2048]{1,0:T(8,128)(2,1)S(1)}, u32[]{:S(2)}, u32[]{:S(2)}) collective-permute-start(bf16[512,2048]{1,0:T(8,128)(2,1)} %sketch_hbm.1), channel_id=1, source_target_pairs={{127,0},{2,1},{1,2},{4,3},{3,4},{6,5},{5,6},{8,7},{7,8},{10,9},{9,... | collective-permute-start | bytes 6291464 | tf_op jit(solution)/shard_map/ppermute | solution.py:363
  18.3 29.4 %collective-permute-start = (bf16[512,2048]{1,0:T(8,128)(2,1)}, bf16[512,2048]{1,0:T(8,128)(2,1)S(1)}, u32[]{:S(2)}, u32[]{:S(2)}) collective-permute-start(bf16[512,2048]{1,0:T(8,128)(2,1)} %sketch_hbm.1), channel_id=1, source_target_pairs={{128,0},{385,1},{130,2},{387,3},{132,4},{389,5},{134,6},{391,7},{1... | collective-permute-start | bytes 6291464 | tf_op jit(solution)/shard_map/ppermute | solution.py:363
  21.0 11.8 %collective-permute-start.3 = (f32[1,2048]{1,0:T(1,128)S(1)}, f32[1,2048]{1,0:T(1,128)S(1)}, u32[]{:S(2)}, u32[]{:S(2)}) collective-permute-start(f32[1,2048]{1,0:T(1,128)S(1)} %get-tuple-element.40), channel_id=1, source_target_pairs={{384,0},{129,1},{386,2},{131,3},{388,4},{133,5},{390,6},{135,7},{3... | collective-permute-start | bytes 24584 | tf_op jit(solution)/shard_map/ppermute | solution.py:363
  25.8 9.9 %collective-permute-start.5 = (f32[1,2048]{1,0:T(1,128)S(1)}, f32[1,2048]{1,0:T(1,128)S(1)}, u32[]{:S(2)}, u32[]{:S(2)}) collective-permute-start(f32[1,2048]{1,0:T(1,128)S(1)} %shard_map.51.d_ref), channel_id=1, source_target_pairs={{510,0},{3,1},{0,2},{5,3},{2,4},{7,5},{4,6},{9,7},{6,8},{11,9},{8,... | collective-permute-start | bytes 24584 | tf_op jit(solution)/shard_map/ppermute | solution.py:363
  27.7 8.0 %collective-permute-start.4 = (f32[1,2048]{1,0:T(1,128)S(1)}, f32[1,2048]{1,0:T(1,128)S(1)}, u32[]{:S(2)}, u32[]{:S(2)}) collective-permute-start(f32[1,2048]{1,0:T(1,128)S(1)} %shard_map.51.d_ref), channel_id=1, source_target_pairs={{129,0},{384,1},{131,2},{386,3},{133,4},{388,5},{135,6},{390,7},{1... | collective-permute-start | bytes 24584 | tf_op jit(solution)/shard_map/ppermute | solution.py:363
  49.8 12.9 %collective-permute-start.7 = (bf16[512,512]{1,0:T(8,128)(2,1)S(1)}, bf16[512,512]{1,0:T(8,128)(2,1)S(1)}, u32[]{:S(2)}, u32[]{:S(2)}) collective-permute-start(bf16[512,512]{1,0:T(8,128)(2,1)S(1)} %get-tuple-element.43.near_block_ref), channel_id=1, source_target_pairs={{0,128},{127,511},{128,256},{255,127},{256,384},{383,255},{384,0},... | collective-permute-start | bytes 1572872 | tf_op jit(solution)/shard_map/ppermute | solution.py:392
  54.5 12.0 %collective-permute-start.6 = (bf16[512,512]{1,0:T(8,128)(2,1)S(1)}, bf16[512,512]{1,0:T(8,128)(2,1)S(1)}, u32[]{:S(2)}, u32[]{:S(2)}) collective-permute-start(bf16[512,512]{1,0:T(8,128)(2,1)S(1)} %get-tuple-element.46), channel_id=1, source_target_pairs={{0,128},{1,385},{2,130},{3,387},{4,132},{5,389},{6,134},{7,391},{8... | collective-permute-start | bytes 1572872 | tf_op jit(solution)/shard_map/ppermute | solution.py:393
  56.5 14.1 %all-to-all-start.1 = ((f32[32,1,128]{2,1,0:T(1,128)}), f32[32,1,128]{2,1,0:T(1,128)S(1)}, u32[]{:S(2)}, u32[]{:S(2)}) async-start(f32[32,1,128]{2,1,0:T(1,128)} %bitcast.7), calls=%async_computation.1 | async-start | bytes 32768 | tf_op jit(solution)/shard_map/all_to_all | solution.py:366
  72.0 0.6 copy-start
  72.0 0.6 copy-start.1

commit v5 on v4

--- a/solution.py
+++ b/solution.py
@@ -81,21 +81,25 @@
     )(sketch, basis)
 
 
-def mate_kernel(mate_ref, u_ref):
+def mate_kernel(mate_ref, own_u_ref, mate_u_ref, both_ref):
     n = mate_ref.shape[0] - EXTRA
     product = jnp.dot(mate_ref[n:, :n], mate_ref[:n, :], preferred_element_type=F32)
-    u_ref[...] = product[0:1, :]
-
-
-def mate_projection(mate):
+    mate_u = product[0:1, :]
+    mate_u_ref[...] = mate_u
+    is_first = lax.axis_index("core") == 0
+    both_ref[0:1, :] = jnp.where(is_first, own_u_ref[...], mate_u)
+    both_ref[1:2, :] = jnp.where(is_first, mate_u, own_u_ref[...])
+
+
+def mate_projection(mate, u):
     return pl.pallas_call(
         mate_kernel,
-        out_shape=shaped((1, mate.shape[1])),
-        in_specs=[whole()],
-        out_specs=whole(),
+        out_shape=(shaped((1, mate.shape[1])), shaped((2, mate.shape[1]))),
+        in_specs=[whole(), whole()],
+        out_specs=(whole(), whole()),
         compiler_params=params(),
         cost_estimate=pl.CostEstimate(flops=2 * mate.size, bytes_accessed=2 * mate.size, transcendentals=0),
-    )(mate)
+    )(mate, u)
 
 
 def column_copy(block_ref, rows_ref, column, sem):
@@ -143,7 +147,9 @@
 
 def image_kernel(sketch_ref, basis_ref, own_ref, a_ref, b_ref, c_ref, d_ref, image_ref, sums_ref):
     rows = own_ref.shape[1]
-    total = (a_ref[...] + b_ref[...]) + (c_ref[...] + d_ref[...])
+    far = a_ref[...] + b_ref[...]
+    far = jnp.where(lax.axis_index("core") == 0, far[0:1, :], far[1:2, :])
+    total = far + (c_ref[...] + d_ref[...])
     high = total.astype(BF16).astype(F32)
     rest = total - high
     middle = rest.astype(BF16).astype(F32)
@@ -373,10 +379,11 @@
     stored = [pltpu.with_memory_space_constraint(array, pltpu.HBM) for array in (sketch, basis)]
     sketch, u, basis = load_and_project(*stored)
     mate = move(sketch, lambda i: i ^ 1)
-    mate_u = mate_projection(mate)
+    mate_u, both_u = mate_projection(mate, u)
+    far_u = move(both_u, lambda i: i - stride if i % 2 == 0 else i + stride)
     parts = (
-        move(u, lambda i: i - stride if i % 2 == 0 else i + stride),
-        move(mate_u, lambda i: i + stride + 1 if i % 2 == 0 else i - stride - 1),
+        far_u,
+        move(far_u, lambda i: i ^ 1),
         move(mate_u, lambda i: i - 2 if i % 2 == 0 else i + 2),
         mate_u,
     )

time: 73.8 us -> 73.8 us (level)
  transfers between devices with their start and end apart: 9 -> 9, of which waited for: 4 -> 3; matrix products, arithmetic and copies ran while one was open for 0% -> 0% of each run, Pallas kernels for 12% -> 12%
where the time goes in v5:
time: 73.8 us; the launch traced here: 72.5 us
  starting transfers between devices  38 us (51%)
  Pallas kernels  12.9 us (17%)
  blocking collectives  10.1 us (14%)
  waiting for transfers between devices  9.49 us (13%)
  between operations  1.46 us (2%)
    ppermute x6, starting transfers between devices, move(): lax.ppermute(block, AXES, [(source_of(i) % devices, i) for i in range(dev...  26.8 us
    all_to_all x1, blocking collectives, trade(): return lax.all_to_all(rows, group, 0, 0, tiled=True)  10.1 us
    all_to_all x1, starting transfers between devices, trade(): return lax.all_to_all(rows, group, 0, 0, tiled=True)  6.17 us
    ppermute x6, waiting for transfers between devices, move(): lax.ppermute(block, AXES, [(source_of(i) % devices, i) for i in range(dev...  3.46 us
    ppermute x1, starting transfers between devices, on_device(): lax.ppermute(near, AXES, [(i, to_sender(i)) for i in corners] + [(2, 4)])  3.08 us
    all_to_all x1, waiting for transfers between devices, trade(): return lax.all_to_all(rows, group, 0, 0, tiled=True)  3.05 us
    ppermute x1, waiting for transfers between devices, on_device(): lax.ppermute(far_back, AXES, [(i, to_sender(i)) for i in range(devices)])  2.98 us
    pallas_call x1, Pallas kernels, own_blocks(): pl.pallas_call(own_blocks_kernel, out_shape=(shaped((n, BANDS * n), BF16)...  2.64 us
  transfers between devices with their start and end apart: 9, of which 3 were waited for; matrix products, arithmetic and copies ran while one was open for 0% of the time, Pallas kernels for 12%

profile of v5, /device:TPU:6, one launch (start us, length us, event | category | flops | bytes accessed | tf_op | source)
XLA Modules:
  0.0 72.5 jit_solution(10658441117381452071)
XLA Ops:
  0.6 1.8 %shard_map.49 = (bf16[528,2048]{1,0:T(8,128)(2,1)S(1)}, f32[1,2048]{1,0:T(1,128)S(1)}, f32[8,512]{1,0:T(8,128)S(1)}) custom-call(bf16[512,2048]{1,0:T(8,128)(2,1)} %sketch_hbm.1, f32[8,512]{1,0:T(8,128)} %basis_hbm.1), custom_call_target="tpu_custom_call" | custom-call | flops 2097152 | tf_op jit(solution)/shard_map/pallas_call | solution.py:71
  2.4 1.9 %collective-permute-start.2 = (bf16[528,2048]{1,0:T(8,128)(2,1)S(1)}, bf16[528,2048]{1,0:T(8,128)(2,1)S(1)}, u32[]{:S(2)}, u32[]{:S(2)}) collective-permute-start(bf16[528,2048]{1,0:T(8,128)(2,1)S(1)} %get-tuple-element.38.sketch_ref), channel_id=1, source_target_pairs={{1,0},{0,1},{3,2},{2,3},{5,4},{4,5},{7,6},{6,7},{9,8},{8,9},{11,10... | collective-permute-start | bytes 6488072 | tf_op jit(solution)/shard_map/ppermute | solution.py:369
  4.3 14.0 %collective-permute-start.1 = (bf16[512,2048]{1,0:T(8,128)(2,1)}, bf16[512,2048]{1,0:T(8,128)(2,1)S(1)}, u32[]{:S(2)}, u32[]{:S(2)}) collective-permute-start(bf16[512,2048]{1,0:T(8,128)(2,1)} %sketch_hbm.1), channel_id=1, source_target_pairs={{127,0},{2,1},{1,2},{4,3},{3,4},{6,5},{5,6},{8,7},{7,8},{10,9},{9,... | collective-permute-start | bytes 6291464 | tf_op jit(solution)/shard_map/ppermute | solution.py:369
  18.3 2.7 %collective-permute-start = (bf16[512,2048]{1,0:T(8,128)(2,1)}, bf16[512,2048]{1,0:T(8,128)(2,1)S(1)}, u32[]{:S(2)}, u32[]{:S(2)}) collective-permute-start(bf16[512,2048]{1,0:T(8,128)(2,1)} %sketch_hbm.1), channel_id=1, source_target_pairs={{128,0},{385,1},{130,2},{387,3},{132,4},{389,5},{134,6},{391,7},{1... | collective-permute-start | bytes 6291464 | tf_op jit(solution)/shard_map/ppermute | solution.py:369
  21.0 0.0 collective-permute-done.2.mate_ref
  21.1 0.4 shard_map.51
  21.4 4.3 %collective-permute-start.3 = (f32[2,2048]{1,0:T(2,128)S(1)}, f32[2,2048]{1,0:T(2,128)S(1)}, u32[]{:S(2)}, u32[]{:S(2)}) collective-permute-start(f32[2,2048]{1,0:T(2,128)S(1)} %get-tuple-element.43), channel_id=1, source_target_pairs={{384,0},{129,1},{386,2},{131,3},{388,4},{133,5},{390,6},{135,7},{3... | collective-permute-start | bytes 49160 | tf_op jit(solution)/shard_map/ppermute | solution.py:369
  25.8 1.9 %collective-permute-start.5 = (f32[1,2048]{1,0:T(1,128)S(1)}, f32[1,2048]{1,0:T(1,128)S(1)}, u32[]{:S(2)}, u32[]{:S(2)}) collective-permute-start(f32[1,2048]{1,0:T(1,128)S(1)} %get-tuple-element.44.d_ref), channel_id=1, source_target_pairs={{510,0},{3,1},{0,2},{5,3},{2,4},{7,5},{4,6},{9,7},{6,8},{11,9},{8,... | collective-permute-start | bytes 24584 | tf_op jit(solution)/shard_map/ppermute | solution.py:369
  27.7 0.0 collective-permute-done.3.a_ref
  27.7 1.9 %collective-permute-start.4 = (f32[2,2048]{1,0:T(2,128)S(1)}, f32[2,2048]{1,0:T(2,128)S(1)}, u32[]{:S(2)}, u32[]{:S(2)}) collective-permute-start(f32[2,2048]{1,0:T(2,128)S(1)} %collective-permute-done.3.a_ref), channel_id=1, source_target_pairs={{1,0},{0,1},{3,2},{2,3},{5,4},{4,5},{7,6},{6,7},{9,8},{8,9},{11,10... | collective-permute-start | bytes 49160 | tf_op jit(solution)/shard_map/ppermute | solution.py:369
  29.6 2.6 %shard_map.50 = (bf16[512,2560]{1,0:T(8,128)(2,1)}, f32[1,512]{1,0:T(1,128)S(1)}, bf16[512,512]{1,0:T(8,128)(2,1)S(1)}) custom-call(bf16[528,2048]{1,0:T(8,128)(2,1)S(1)} %get-tuple-element.38.sketch_ref, bf16[528,2048]{1,0:T(8,128)(2,1)S(1)} %collective-permute-done.2.mate_ref, f32[8,512]{1,0:T(8,128)S(1)} %get-tuple-element.39.basis_ref), custom_call_target="tpu_custom_call" | custom-call | flops 2147483648 | bytes 2097152 | tf_op jit(solution)/shard_map/pallas_call | solution.py:135
  32.3 3.4 %collective-permute-done.5.c_ref = f32[1,2048]{1,0:T(1,128)S(1)} collective-permute-done((f32[1,2048]{1,0:T(1,128)S(1)}, f32[1,2048]{1,0:T(1,128)S(1)}, u32[]{:S(2)}, u32[]{:S(2)}) %collective-permute-start.5) | collective-permute-done | bytes 8224 | tf_op jit(solution)/shard_map/ppermute | solution.py:369
  35.7 0.0 collective-permute-done.4.b_ref
  35.7 1.2 %shard_map.52 = (f32[1,512]{1,0:T(1,128)S(1)}, f32[16,128]{1,0:T(8,128)S(1)}) custom-call(bf16[528,2048]{1,0:T(8,128)(2,1)S(1)} %get-tuple-element.38.sketch_ref, f32[8,512]{1,0:T(8,128)S(1)} %get-tuple-element.39.basis_ref, f32[1,512]{1,0:T(1,128)S(1)} %get-tuple-element.41.own_ref, f32[2,2048]{1,0:T(2,128)S(1)} %collective-permute-done.3.a_ref, ...), custom_call_target="tpu_custom_call" | custom-call | flops 33554432 | bytes 2097152 | tf_op jit(solution)/shard_map/pallas_call | solution.py:178
  36.9 10.1 %all_to_all.22 = f32[16,1,128]{2,1,0:T(1,128)S(1)} all-to-all(f32[16,1,128]{2,1,0:T(1,128)S(1)} %bitcast.17), channel_id=1, replica_groups=mesh['x'=4,'z'=8,'y'=8,'core'=2] {'z','core'}, dimensions={0} | all-to-all | bytes 16384 | tf_op jit(solution)/shard_map/all_to_all | solution.py:372
  47.0 0.6 shard_map.53.token_ref
  47.6 0.0 collective-permute-done.1.near_ref
  47.6 0.0 collective-permute-done.far_ref
  47.6 2.0 %shard_map.54 = (bf16[512,2560]{1,0:T(8,128)(2,1)}, bf16[512,512]{1,0:T(8,128)(2,1)S(1)}) custom-call(bf16[528,2048]{1,0:T(8,128)(2,1)S(1)} %get-tuple-element.38.sketch_ref, bf16[512,2048]{1,0:T(8,128)(2,1)S(1)} %collective-permute-done.far_ref, bf16[512,2048]{1,0:T(8,128)(2,1)S(1)} %collective-permute-done.1.near_ref, ...), custom_call_target="tpu_custom_call", output_to_operand_aliasing={{0}: (5, {})} | custom-call | flops 1073741824 | bytes 4194304 | tf_op jit(solution)/shard_map/pallas_call | solution.py:227
  49.7 3.1 %collective-permute-start.7 = (bf16[512,512]{1,0:T(8,128)(2,1)S(1)}, bf16[512,512]{1,0:T(8,128)(2,1)S(1)}, u32[]{:S(2)}, u32[]{:S(2)}) collective-permute-start(bf16[512,512]{1,0:T(8,128)(2,1)S(1)} %get-tuple-element.47.near_block_ref), channel_id=1, source_target_pairs={{0,128},{127,511},{128,256},{255,127},{256,384},{383,255},{384,0},... | collective-permute-start | bytes 1572872 | tf_op jit(solution)/shard_map/ppermute | solution.py:399
  52.8 1.8 %shard_map.55 = (bf16[512,2560]{1,0:T(8,128)(2,1)}, bf16[512,512]{1,0:T(8,128)(2,1)S(1)}, bf16[512,512]{1,0:T(8,128)(2,1)S(1)}) custom-call(bf16[528,2048]{1,0:T(8,128)(2,1)S(1)} %get-tuple-element.38.sketch_ref, bf16[512,2048]{1,0:T(8,128)(2,1)S(1)} %collective-permute-done.far_ref, ...), custom_call_target="tpu_custom_call", output_to_operand_aliasing={{0}: (3, {})} | custom-call | flops 1073741824 | bytes 4194304 | tf_op jit(solution)/shard_map/pallas_call | solution.py:254
  54.5 1.9 %collective-permute-start.6 = (bf16[512,512]{1,0:T(8,128)(2,1)S(1)}, bf16[512,512]{1,0:T(8,128)(2,1)S(1)}, u32[]{:S(2)}, u32[]{:S(2)}) collective-permute-start(bf16[512,512]{1,0:T(8,128)(2,1)S(1)} %get-tuple-element.50), channel_id=1, source_target_pairs={{0,128},{1,385},{2,130},{3,387},{4,132},{5,389},{6,134},{7,391},{8... | collective-permute-start | bytes 1572872 | tf_op jit(solution)/shard_map/ppermute | solution.py:400
  56.5 6.2 %all-to-all-start.1 = ((f32[32,1,128]{2,1,0:T(1,128)}), f32[32,1,128]{2,1,0:T(1,128)S(1)}, u32[]{:S(2)}, u32[]{:S(2)}) async-start(f32[32,1,128]{2,1,0:T(1,128)} %bitcast.7), calls=%async_computation.1 | async-start | bytes 32768 | tf_op jit(solution)/shard_map/all_to_all | solution.py:372
  62.6 0.0 collective-permute-done.7.corner_ref
  62.7 0.8 %shard_map.56.rows_in_ref = bf16[512,2560]{1,0:T(8,128)(2,1)} custom-call(bf16[512,512]{1,0:T(8,128)(2,1)S(1)} %collective-permute-done.7.corner_ref, bf16[512,2560]{1,0:T(8,128)(2,1)} %get-tuple-element.51.rows_in_ref), custom_call_target="tpu_custom_call", output_to_operand_aliasing={{}: (1, {})} | custom-call | bytes 524288 | tf_op jit(solution)/shard_map/pallas_call | solution.py:280
  63.5 3.0 %collective-permute-done.6.back_ref = bf16[512,512]{1,0:T(8,128)(2,1)S(1)} collective-permute-done((bf16[512,512]{1,0:T(8,128)(2,1)S(1)}, bf16[512,512]{1,0:T(8,128)(2,1)S(1)}, u32[]{:S(2)}, u32[]{:S(2)}) %collective-permute-start.6) | collective-permute-done | bytes 524320 | tf_op jit(solution)/shard_map/ppermute | solution.py:400
  66.5 1.0 %shard_map.57 = (bf16[512,2560]{1,0:T(8,128)(2,1)}, f32[8,128]{1,0:T(8,128)S(1)}) custom-call(bf16[512,512]{1,0:T(8,128)(2,1)S(1)} %get-tuple-element.49.far_ref, bf16[512,512]{1,0:T(8,128)(2,1)S(1)} %collective-permute-done.6.back_ref, bf16[512,2560]{1,0:T(8,128)(2,1)} %shard_map.56.rows_in_ref), custom_call_target="tpu_custom_call", output_to_operand_aliasing={{0}: (2, {})} | custom-call | bytes 2097152 | tf_op jit(solution)/shard_map/pallas_call | solution.py:305
  67.4 3.0 %all-to-all-done.1 = f32[32,1,128]{2,1,0:T(1,128)S(1)} async-done(((f32[32,1,128]{2,1,0:T(1,128)}), f32[32,1,128]{2,1,0:T(1,128)S(1)}, u32[]{:S(2)}, u32[]{:S(2)}) %all-to-all-start.1) | async-done | bytes 16416 | tf_op jit(solution)/shard_map/all_to_all | solution.py:372
  70.5 0.7 %shard_map.58 = (f32[1,512]{1,0:T(1,128)S(1)}, f32[1,512]{1,0:T(1,128)S(1)}, f32[1,128]{1,0:T(1,128)S(1)}, s32[1]{0:T(128)}) custom-call(f32[32,128]{1,0:T(8,128)S(1)} %bitcast.15, f32[8,512]{1,0:T(8,128)S(1)} %get-tuple-element.39.basis_ref, f32[1,512]{1,0:T(1,128)S(1)} %get-tuple-element.53.image_ref, f32[8,128]{1,0:T(8,128)S(1)} %get-tuple-element.54.token_ref), custom_call_target="tpu_custom_call" | custom-call | tf_op jit(solution)/shard_map/pallas_call | solution.py:347
  71.9 0.0 copy-start
  71.9 0.0 copy-start.1
  71.9 0.6 copy-done
  72.5 0.0 copy-done.1
  (2 shorter events, 0.0 us)
Async XLA Ops:
  2.4 18.6 %collective-permute-start.2 = (bf16[528,2048]{1,0:T(8,128)(2,1)S(1)}, bf16[528,2048]{1,0:T(8,128)(2,1)S(1)}, u32[]{:S(2)}, u32[]{:S(2)}) collective-permute-start(bf16[528,2048]{1,0:T(8,128)(2,1)S(1)} %get-tuple-element.38.sketch_ref), channel_id=1, source_target_pairs={{1,0},{0,1},{3,2},{2,3},{5,4},{4,5},{7,6},{6,7},{9,8},{8,9},{11,10... | collective-permute-start | bytes 6488072 | tf_op jit(solution)/shard_map/ppermute | solution.py:369
  4.3 43.3 %collective-permute-start.1 = (bf16[512,2048]{1,0:T(8,128)(2,1)}, bf16[512,2048]{1,0:T(8,128)(2,1)S(1)}, u32[]{:S(2)}, u32[]{:S(2)}) collective-permute-start(bf16[512,2048]{1,0:T(8,128)(2,1)} %sketch_hbm.1), channel_id=1, source_target_pairs={{127,0},{2,1},{1,2},{4,3},{3,4},{6,5},{5,6},{8,7},{7,8},{10,9},{9,... | collective-permute-start | bytes 6291464 | tf_op jit(solution)/shard_map/ppermute | solution.py:369
  18.3 29.4 %collective-permute-start = (bf16[512,2048]{1,0:T(8,128)(2,1)}, bf16[512,2048]{1,0:T(8,128)(2,1)S(1)}, u32[]{:S(2)}, u32[]{:S(2)}) collective-permute-start(bf16[512,2048]{1,0:T(8,128)(2,1)} %sketch_hbm.1), channel_id=1, source_target_pairs={{128,0},{385,1},{130,2},{387,3},{132,4},{389,5},{134,6},{391,7},{1... | collective-permute-start | bytes 6291464 | tf_op jit(solution)/shard_map/ppermute | solution.py:369
  21.4 6.3 %collective-permute-start.3 = (f32[2,2048]{1,0:T(2,128)S(1)}, f32[2,2048]{1,0:T(2,128)S(1)}, u32[]{:S(2)}, u32[]{:S(2)}) collective-permute-start(f32[2,2048]{1,0:T(2,128)S(1)} %get-tuple-element.43), channel_id=1, source_target_pairs={{384,0},{129,1},{386,2},{131,3},{388,4},{133,5},{390,6},{135,7},{3... | collective-permute-start | bytes 49160 | tf_op jit(solution)/shard_map/ppermute | solution.py:369
  25.8 9.9 %collective-permute-start.5 = (f32[1,2048]{1,0:T(1,128)S(1)}, f32[1,2048]{1,0:T(1,128)S(1)}, u32[]{:S(2)}, u32[]{:S(2)}) collective-permute-start(f32[1,2048]{1,0:T(1,128)S(1)} %get-tuple-element.44.d_ref), channel_id=1, source_target_pairs={{510,0},{3,1},{0,2},{5,3},{2,4},{7,5},{4,6},{9,7},{6,8},{11,9},{8,... | collective-permute-start | bytes 24584 | tf_op jit(solution)/shard_map/ppermute | solution.py:369
  27.7 8.0 %collective-permute-start.4 = (f32[2,2048]{1,0:T(2,128)S(1)}, f32[2,2048]{1,0:T(2,128)S(1)}, u32[]{:S(2)}, u32[]{:S(2)}) collective-permute-start(f32[2,2048]{1,0:T(2,128)S(1)} %collective-permute-done.3.a_ref), channel_id=1, source_target_pairs={{1,0},{0,1},{3,2},{2,3},{5,4},{4,5},{7,6},{6,7},{9,8},{8,9},{11,10... | collective-permute-start | bytes 49160 | tf_op jit(solution)/shard_map/ppermute | solution.py:369
  49.7 13.0 %collective-permute-start.7 = (bf16[512,512]{1,0:T(8,128)(2,1)S(1)}, bf16[512,512]{1,0:T(8,128)(2,1)S(1)}, u32[]{:S(2)}, u32[]{:S(2)}) collective-permute-start(bf16[512,512]{1,0:T(8,128)(2,1)S(1)} %get-tuple-element.47.near_block_ref), channel_id=1, source_target_pairs={{0,128},{127,511},{128,256},{255,127},{256,384},{383,255},{384,0},... | collective-permute-start | bytes 1572872 | tf_op jit(solution)/shard_map/ppermute | solution.py:399
  54.5 11.9 %collective-permute-start.6 = (bf16[512,512]{1,0:T(8,128)(2,1)S(1)}, bf16[512,512]{1,0:T(8,128)(2,1)S(1)}, u32[]{:S(2)}, u32[]{:S(2)}) collective-permute-start(bf16[512,512]{1,0:T(8,128)(2,1)S(1)} %get-tuple-element.50), channel_id=1, source_target_pairs={{0,128},{1,385},{2,130},{3,387},{4,132},{5,389},{6,134},{7,391},{8... | collective-permute-start | bytes 1572872 | tf_op jit(solution)/shard_map/ppermute | solution.py:400
  56.5 14.0 %all-to-all-start.1 = ((f32[32,1,128]{2,1,0:T(1,128)}), f32[32,1,128]{2,1,0:T(1,128)S(1)}, u32[]{:S(2)}, u32[]{:S(2)}) async-start(f32[32,1,128]{2,1,0:T(1,128)} %bitcast.7), calls=%async_computation.1 | async-start | bytes 32768 | tf_op jit(solution)/shard_map/all_to_all | solution.py:372
  71.9 0.6 copy-start
  71.9 0.6 copy-start.1

commit v6 on v5

--- a/solution.py
+++ b/solution.py
@@ -211,13 +211,8 @@
     rank, last = plane_rank()
     is_corner = (rank == 0) | (rank == last)
 
-    @pl.when(is_corner)
-    def _():
-        block_ref[...] = dot_last(far_ref[...], near_ref[...]).astype(BF16)
-
-    @pl.when(jnp.logical_not(is_corner))
-    def _():
-        block_ref[...] = dot_last(sketch_ref[: block_ref.shape[0], :], near_ref[...]).astype(BF16)
+    left = jnp.where(is_corner, far_ref[...], sketch_ref[: block_ref.shape[0], :])
+    block_ref[...] = dot_last(left, near_ref[...]).astype(BF16)
 
     copy.wait()
 

time: 73.8 us -> 73.8 us (level)
  no operation moved by 1% of the time
where the time goes in v6:
time: 73.8 us; the launch traced here: 72.5 us
  starting transfers between devices  38 us (51%)
  Pallas kernels  12.9 us (17%)
  blocking collectives  10.1 us (14%)
  waiting for transfers between devices  9.49 us (13%)
  between operations  1.46 us (2%)
    ppermute x6, starting transfers between devices, move(): lax.ppermute(block, AXES, [(source_of(i) % devices, i) for i in range(dev...  26.8 us
    all_to_all x1, blocking collectives, trade(): return lax.all_to_all(rows, group, 0, 0, tiled=True)  10.1 us
    all_to_all x1, starting transfers between devices, trade(): return lax.all_to_all(rows, group, 0, 0, tiled=True)  6.17 us
    ppermute x6, waiting for transfers between devices, move(): lax.ppermute(block, AXES, [(source_of(i) % devices, i) for i in range(dev...  3.46 us
    ppermute x1, starting transfers between devices, on_device(): lax.ppermute(near, AXES, [(i, to_sender(i)) for i in corners] + [(2, 4)])  3.09 us
    all_to_all x1, waiting for transfers between devices, trade(): return lax.all_to_all(rows, group, 0, 0, tiled=True)  3.06 us
    ppermute x1, waiting for transfers between devices, on_device(): lax.ppermute(far_back, AXES, [(i, to_sender(i)) for i in range(devices)])  2.97 us
    pallas_call x1, Pallas kernels, own_blocks(): pl.pallas_call(own_blocks_kernel, out_shape=(shaped((n, BANDS * n), BF16)...  2.64 us
  transfers between devices with their start and end apart: 9, of which 3 were waited for; matrix products, arithmetic and copies ran while one was open for 0% of the time, Pallas kernels for 12%

profile of v6, /device:TPU:6, one launch (start us, length us, event | category | flops | bytes accessed | tf_op | source)
XLA Modules:
  0.0 72.5 jit_solution(3174279362164350761)
XLA Ops:
  0.6 1.8 %shard_map.49 = (bf16[528,2048]{1,0:T(8,128)(2,1)S(1)}, f32[1,2048]{1,0:T(1,128)S(1)}, f32[8,512]{1,0:T(8,128)S(1)}) custom-call(bf16[512,2048]{1,0:T(8,128)(2,1)} %sketch_hbm.1, f32[8,512]{1,0:T(8,128)} %basis_hbm.1), custom_call_target="tpu_custom_call" | custom-call | flops 2097152 | tf_op jit(solution)/shard_map/pallas_call | solution.py:71
  2.4 1.9 %collective-permute-start.2 = (bf16[528,2048]{1,0:T(8,128)(2,1)S(1)}, bf16[528,2048]{1,0:T(8,128)(2,1)S(1)}, u32[]{:S(2)}, u32[]{:S(2)}) collective-permute-start(bf16[528,2048]{1,0:T(8,128)(2,1)S(1)} %get-tuple-element.38.sketch_ref), channel_id=1, source_target_pairs={{1,0},{0,1},{3,2},{2,3},{5,4},{4,5},{7,6},{6,7},{9,8},{8,9},{11,10... | collective-permute-start | bytes 6488072 | tf_op jit(solution)/shard_map/ppermute | solution.py:364
  4.3 14.0 %collective-permute-start.1 = (bf16[512,2048]{1,0:T(8,128)(2,1)}, bf16[512,2048]{1,0:T(8,128)(2,1)S(1)}, u32[]{:S(2)}, u32[]{:S(2)}) collective-permute-start(bf16[512,2048]{1,0:T(8,128)(2,1)} %sketch_hbm.1), channel_id=1, source_target_pairs={{127,0},{2,1},{1,2},{4,3},{3,4},{6,5},{5,6},{8,7},{7,8},{10,9},{9,... | collective-permute-start | bytes 6291464 | tf_op jit(solution)/shard_map/ppermute | solution.py:364
  18.3 2.7 %collective-permute-start = (bf16[512,2048]{1,0:T(8,128)(2,1)}, bf16[512,2048]{1,0:T(8,128)(2,1)S(1)}, u32[]{:S(2)}, u32[]{:S(2)}) collective-permute-start(bf16[512,2048]{1,0:T(8,128)(2,1)} %sketch_hbm.1), channel_id=1, source_target_pairs={{128,0},{385,1},{130,2},{387,3},{132,4},{389,5},{134,6},{391,7},{1... | collective-permute-start | bytes 6291464 | tf_op jit(solution)/shard_map/ppermute | solution.py:364
  21.0 0.0 collective-permute-done.2.mate_ref
  21.1 0.4 shard_map.51
  21.4 4.3 %collective-permute-start.3 = (f32[2,2048]{1,0:T(2,128)S(1)}, f32[2,2048]{1,0:T(2,128)S(1)}, u32[]{:S(2)}, u32[]{:S(2)}) collective-permute-start(f32[2,2048]{1,0:T(2,128)S(1)} %get-tuple-element.43), channel_id=1, source_target_pairs={{384,0},{129,1},{386,2},{131,3},{388,4},{133,5},{390,6},{135,7},{3... | collective-permute-start | bytes 49160 | tf_op jit(solution)/shard_map/ppermute | solution.py:364
  25.8 1.9 %collective-permute-start.5 = (f32[1,2048]{1,0:T(1,128)S(1)}, f32[1,2048]{1,0:T(1,128)S(1)}, u32[]{:S(2)}, u32[]{:S(2)}) collective-permute-start(f32[1,2048]{1,0:T(1,128)S(1)} %get-tuple-element.44.d_ref), channel_id=1, source_target_pairs={{510,0},{3,1},{0,2},{5,3},{2,4},{7,5},{4,6},{9,7},{6,8},{11,9},{8,... | collective-permute-start | bytes 24584 | tf_op jit(solution)/shard_map/ppermute | solution.py:364
  27.7 0.0 collective-permute-done.3.a_ref
  27.7 1.9 %collective-permute-start.4 = (f32[2,2048]{1,0:T(2,128)S(1)}, f32[2,2048]{1,0:T(2,128)S(1)}, u32[]{:S(2)}, u32[]{:S(2)}) collective-permute-start(f32[2,2048]{1,0:T(2,128)S(1)} %collective-permute-done.3.a_ref), channel_id=1, source_target_pairs={{1,0},{0,1},{3,2},{2,3},{5,4},{4,5},{7,6},{6,7},{9,8},{8,9},{11,10... | collective-permute-start | bytes 49160 | tf_op jit(solution)/shard_map/ppermute | solution.py:364
  29.6 2.6 %shard_map.50 = (bf16[512,2560]{1,0:T(8,128)(2,1)}, f32[1,512]{1,0:T(1,128)S(1)}, bf16[512,512]{1,0:T(8,128)(2,1)S(1)}) custom-call(bf16[528,2048]{1,0:T(8,128)(2,1)S(1)} %get-tuple-element.38.sketch_ref, bf16[528,2048]{1,0:T(8,128)(2,1)S(1)} %collective-permute-done.2.mate_ref, f32[8,512]{1,0:T(8,128)S(1)} %get-tuple-element.39.basis_ref), custom_call_target="tpu_custom_call" | custom-call | flops 2147483648 | bytes 2097152 | tf_op jit(solution)/shard_map/pallas_call | solution.py:135
  32.3 3.4 %collective-permute-done.5.c_ref = f32[1,2048]{1,0:T(1,128)S(1)} collective-permute-done((f32[1,2048]{1,0:T(1,128)S(1)}, f32[1,2048]{1,0:T(1,128)S(1)}, u32[]{:S(2)}, u32[]{:S(2)}) %collective-permute-start.5) | collective-permute-done | bytes 8224 | tf_op jit(solution)/shard_map/ppermute | solution.py:364
  35.7 0.0 collective-permute-done.4.b_ref
  35.7 1.2 %shard_map.52 = (f32[1,512]{1,0:T(1,128)S(1)}, f32[16,128]{1,0:T(8,128)S(1)}) custom-call(bf16[528,2048]{1,0:T(8,128)(2,1)S(1)} %get-tuple-element.38.sketch_ref, f32[8,512]{1,0:T(8,128)S(1)} %get-tuple-element.39.basis_ref, f32[1,512]{1,0:T(1,128)S(1)} %get-tuple-element.41.own_ref, f32[2,2048]{1,0:T(2,128)S(1)} %collective-permute-done.3.a_ref, ...), custom_call_target="tpu_custom_call" | custom-call | flops 33554432 | bytes 2097152 | tf_op jit(solution)/shard_map/pallas_call | solution.py:178
  36.9 10.1 %all_to_all.22 = f32[16,1,128]{2,1,0:T(1,128)S(1)} all-to-all(f32[16,1,128]{2,1,0:T(1,128)S(1)} %bitcast.17), channel_id=1, replica_groups=mesh['x'=4,'z'=8,'y'=8,'core'=2] {'z','core'}, dimensions={0} | all-to-all | bytes 16384 | tf_op jit(solution)/shard_map/all_to_all | solution.py:367
  47.0 0.6 shard_map.53.token_ref
  47.6 0.0 collective-permute-done.1.near_ref
  47.6 0.0 collective-permute-done.far_ref
  47.6 2.0 %shard_map.54 = (bf16[512,2560]{1,0:T(8,128)(2,1)}, bf16[512,512]{1,0:T(8,128)(2,1)S(1)}) custom-call(bf16[528,2048]{1,0:T(8,128)(2,1)S(1)} %get-tuple-element.38.sketch_ref, bf16[512,2048]{1,0:T(8,128)(2,1)S(1)} %collective-permute-done.far_ref, bf16[512,2048]{1,0:T(8,128)(2,1)S(1)} %collective-permute-done.1.near_ref, ...), custom_call_target="tpu_custom_call", output_to_operand_aliasing={{0}: (5, {})} | custom-call | flops 1073741824 | bytes 4194304 | tf_op jit(solution)/shard_map/pallas_call | solution.py:222
  49.7 3.1 %collective-permute-start.7 = (bf16[512,512]{1,0:T(8,128)(2,1)S(1)}, bf16[512,512]{1,0:T(8,128)(2,1)S(1)}, u32[]{:S(2)}, u32[]{:S(2)}) collective-permute-start(bf16[512,512]{1,0:T(8,128)(2,1)S(1)} %get-tuple-element.47.near_block_ref), channel_id=1, source_target_pairs={{0,128},{127,511},{128,256},{255,127},{256,384},{383,255},{384,0},... | collective-permute-start | bytes 1572872 | tf_op jit(solution)/shard_map/ppermute | solution.py:394
  52.8 1.8 %shard_map.55 = (bf16[512,2560]{1,0:T(8,128)(2,1)}, bf16[512,512]{1,0:T(8,128)(2,1)S(1)}, bf16[512,512]{1,0:T(8,128)(2,1)S(1)}) custom-call(bf16[528,2048]{1,0:T(8,128)(2,1)S(1)} %get-tuple-element.38.sketch_ref, bf16[512,2048]{1,0:T(8,128)(2,1)S(1)} %collective-permute-done.far_ref, ...), custom_call_target="tpu_custom_call", output_to_operand_aliasing={{0}: (3, {})} | custom-call | flops 1073741824 | bytes 4194304 | tf_op jit(solution)/shard_map/pallas_call | solution.py:249
  54.5 1.9 %collective-permute-start.6 = (bf16[512,512]{1,0:T(8,128)(2,1)S(1)}, bf16[512,512]{1,0:T(8,128)(2,1)S(1)}, u32[]{:S(2)}, u32[]{:S(2)}) collective-permute-start(bf16[512,512]{1,0:T(8,128)(2,1)S(1)} %get-tuple-element.50), channel_id=1, source_target_pairs={{0,128},{1,385},{2,130},{3,387},{4,132},{5,389},{6,134},{7,391},{8... | collective-permute-start | bytes 1572872 | tf_op jit(solution)/shard_map/ppermute | solution.py:395
  56.5 6.2 %all-to-all-start.1 = ((f32[32,1,128]{2,1,0:T(1,128)}), f32[32,1,128]{2,1,0:T(1,128)S(1)}, u32[]{:S(2)}, u32[]{:S(2)}) async-start(f32[32,1,128]{2,1,0:T(1,128)} %bitcast.7), calls=%async_computation.1 | async-start | bytes 32768 | tf_op jit(solution)/shard_map/all_to_all | solution.py:367
  62.7 0.0 collective-permute-done.7.corner_ref
  62.7 0.8 %shard_map.56.rows_in_ref = bf16[512,2560]{1,0:T(8,128)(2,1)} custom-call(bf16[512,512]{1,0:T(8,128)(2,1)S(1)} %collective-permute-done.7.corner_ref, bf16[512,2560]{1,0:T(8,128)(2,1)} %get-tuple-element.51.rows_in_ref), custom_call_target="tpu_custom_call", output_to_operand_aliasing={{}: (1, {})} | custom-call | bytes 524288 | tf_op jit(solution)/shard_map/pallas_call | solution.py:275
  63.5 3.0 %collective-permute-done.6.back_ref = bf16[512,512]{1,0:T(8,128)(2,1)S(1)} collective-permute-done((bf16[512,512]{1,0:T(8,128)(2,1)S(1)}, bf16[512,512]{1,0:T(8,128)(2,1)S(1)}, u32[]{:S(2)}, u32[]{:S(2)}) %collective-permute-start.6) | collective-permute-done | bytes 524320 | tf_op jit(solution)/shard_map/ppermute | solution.py:395
  66.5 1.0 %shard_map.57 = (bf16[512,2560]{1,0:T(8,128)(2,1)}, f32[8,128]{1,0:T(8,128)S(1)}) custom-call(bf16[512,512]{1,0:T(8,128)(2,1)S(1)} %get-tuple-element.49.far_ref, bf16[512,512]{1,0:T(8,128)(2,1)S(1)} %collective-permute-done.6.back_ref, bf16[512,2560]{1,0:T(8,128)(2,1)} %shard_map.56.rows_in_ref), custom_call_target="tpu_custom_call", output_to_operand_aliasing={{0}: (2, {})} | custom-call | bytes 2097152 | tf_op jit(solution)/shard_map/pallas_call | solution.py:300
  67.5 3.1 %all-to-all-done.1 = f32[32,1,128]{2,1,0:T(1,128)S(1)} async-done(((f32[32,1,128]{2,1,0:T(1,128)}), f32[32,1,128]{2,1,0:T(1,128)S(1)}, u32[]{:S(2)}, u32[]{:S(2)}) %all-to-all-start.1) | async-done | bytes 16416 | tf_op jit(solution)/shard_map/all_to_all | solution.py:367
  70.5 0.7 %shard_map.58 = (f32[1,512]{1,0:T(1,128)S(1)}, f32[1,512]{1,0:T(1,128)S(1)}, f32[1,128]{1,0:T(1,128)S(1)}, s32[1]{0:T(128)}) custom-call(f32[32,128]{1,0:T(8,128)S(1)} %bitcast.15, f32[8,512]{1,0:T(8,128)S(1)} %get-tuple-element.39.basis_ref, f32[1,512]{1,0:T(1,128)S(1)} %get-tuple-element.53.image_ref, f32[8,128]{1,0:T(8,128)S(1)} %get-tuple-element.54.token_ref), custom_call_target="tpu_custom_call" | custom-call | tf_op jit(solution)/shard_map/pallas_call | solution.py:342
  71.9 0.0 copy-start
  71.9 0.0 copy-start.1
  71.9 0.6 copy-done
  72.5 0.0 copy-done.1
  (2 shorter events, 0.0 us)
Async XLA Ops:
  2.4 18.6 %collective-permute-start.2 = (bf16[528,2048]{1,0:T(8,128)(2,1)S(1)}, bf16[528,2048]{1,0:T(8,128)(2,1)S(1)}, u32[]{:S(2)}, u32[]{:S(2)}) collective-permute-start(bf16[528,2048]{1,0:T(8,128)(2,1)S(1)} %get-tuple-element.38.sketch_ref), channel_id=1, source_target_pairs={{1,0},{0,1},{3,2},{2,3},{5,4},{4,5},{7,6},{6,7},{9,8},{8,9},{11,10... | collective-permute-start | bytes 6488072 | tf_op jit(solution)/shard_map/ppermute | solution.py:364
  4.3 43.3 %collective-permute-start.1 = (bf16[512,2048]{1,0:T(8,128)(2,1)}, bf16[512,2048]{1,0:T(8,128)(2,1)S(1)}, u32[]{:S(2)}, u32[]{:S(2)}) collective-permute-start(bf16[512,2048]{1,0:T(8,128)(2,1)} %sketch_hbm.1), channel_id=1, source_target_pairs={{127,0},{2,1},{1,2},{4,3},{3,4},{6,5},{5,6},{8,7},{7,8},{10,9},{9,... | collective-permute-start | bytes 6291464 | tf_op jit(solution)/shard_map/ppermute | solution.py:364
  18.3 29.4 %collective-permute-start = (bf16[512,2048]{1,0:T(8,128)(2,1)}, bf16[512,2048]{1,0:T(8,128)(2,1)S(1)}, u32[]{:S(2)}, u32[]{:S(2)}) collective-permute-start(bf16[512,2048]{1,0:T(8,128)(2,1)} %sketch_hbm.1), channel_id=1, source_target_pairs={{128,0},{385,1},{130,2},{387,3},{132,4},{389,5},{134,6},{391,7},{1... | collective-permute-start | bytes 6291464 | tf_op jit(solution)/shard_map/ppermute | solution.py:364
  21.4 6.3 %collective-permute-start.3 = (f32[2,2048]{1,0:T(2,128)S(1)}, f32[2,2048]{1,0:T(2,128)S(1)}, u32[]{:S(2)}, u32[]{:S(2)}) collective-permute-start(f32[2,2048]{1,0:T(2,128)S(1)} %get-tuple-element.43), channel_id=1, source_target_pairs={{384,0},{129,1},{386,2},{131,3},{388,4},{133,5},{390,6},{135,7},{3... | collective-permute-start | bytes 49160 | tf_op jit(solution)/shard_map/ppermute | solution.py:364
  25.8 9.9 %collective-permute-start.5 = (f32[1,2048]{1,0:T(1,128)S(1)}, f32[1,2048]{1,0:T(1,128)S(1)}, u32[]{:S(2)}, u32[]{:S(2)}) collective-permute-start(f32[1,2048]{1,0:T(1,128)S(1)} %get-tuple-element.44.d_ref), channel_id=1, source_target_pairs={{510,0},{3,1},{0,2},{5,3},{2,4},{7,5},{4,6},{9,7},{6,8},{11,9},{8,... | collective-permute-start | bytes 24584 | tf_op jit(solution)/shard_map/ppermute | solution.py:364
  27.7 8.0 %collective-permute-start.4 = (f32[2,2048]{1,0:T(2,128)S(1)}, f32[2,2048]{1,0:T(2,128)S(1)}, u32[]{:S(2)}, u32[]{:S(2)}) collective-permute-start(f32[2,2048]{1,0:T(2,128)S(1)} %collective-permute-done.3.a_ref), channel_id=1, source_target_pairs={{1,0},{0,1},{3,2},{2,3},{5,4},{4,5},{7,6},{6,7},{9,8},{8,9},{11,10... | collective-permute-start | bytes 49160 | tf_op jit(solution)/shard_map/ppermute | solution.py:364
  49.7 13.0 %collective-permute-start.7 = (bf16[512,512]{1,0:T(8,128)(2,1)S(1)}, bf16[512,512]{1,0:T(8,128)(2,1)S(1)}, u32[]{:S(2)}, u32[]{:S(2)}) collective-permute-start(bf16[512,512]{1,0:T(8,128)(2,1)S(1)} %get-tuple-element.47.near_block_ref), channel_id=1, source_target_pairs={{0,128},{127,511},{128,256},{255,127},{256,384},{383,255},{384,0},... | collective-permute-start | bytes 1572872 | tf_op jit(solution)/shard_map/ppermute | solution.py:394
  54.5 11.9 %collective-permute-start.6 = (bf16[512,512]{1,0:T(8,128)(2,1)S(1)}, bf16[512,512]{1,0:T(8,128)(2,1)S(1)}, u32[]{:S(2)}, u32[]{:S(2)}) collective-permute-start(bf16[512,512]{1,0:T(8,128)(2,1)S(1)} %get-tuple-element.50), channel_id=1, source_target_pairs={{0,128},{1,385},{2,130},{3,387},{4,132},{5,389},{6,134},{7,391},{8... | collective-permute-start | bytes 1572872 | tf_op jit(solution)/shard_map/ppermute | solution.py:395
  56.5 14.0 %all-to-all-start.1 = ((f32[32,1,128]{2,1,0:T(1,128)}), f32[32,1,128]{2,1,0:T(1,128)S(1)}, u32[]{:S(2)}, u32[]{:S(2)}) async-start(f32[32,1,128]{2,1,0:T(1,128)} %bitcast.7), calls=%async_computation.1 | async-start | bytes 32768 | tf_op jit(solution)/shard_map/all_to_all | solution.py:367
  71.9 0.6 copy-start
  71.9 0.6 copy-start.1
